TPU v7x, 768 devices: a whole 4x8x12 slice. The times are simulated.
768 devices in a mesh: dp: 4 (over x), ctx: 32 (over z_hi, y), mp: 6 (over z_lo, core).
Axes of the slice: x: 4, y: 8, z: 12 (z_hi: 4, z_lo: 3; z = z_hi * 3 + z_lo), core: 2. Of those that a mesh axis runs over, the one named last changes fastest.
Arguments:
- streams: bfloat16 [16384, 3, 4608], P(('dp', 'ctx'), None, 'mp'), parts along dimension 0, may hold values from -6 to 6
- short_taps: float32 [7, 3, 288], P(None, None, 'mp'), may hold values from -2.5 to 2.5
- modal_residue: float32 [16, 288], P(None, 'mp'), may hold values from -0.09 to 0.09
- modal_rate: float32 [16, 288], P(None, 'mp'), may hold values from 1.2207031e-05 to 0.03
- skip_gain: float32 [4608], P('mp'), may hold values from -4 to 4
- queries: bfloat16 [16384, 48, 128], P(('dp', 'ctx'), 'mp'), parts along dimension 0, may hold values from -9 to 9
- keys: bfloat16 [16384, 6, 128], P(('dp', 'ctx'), 'mp'), parts along dimension 0, may hold values from -9 to 9
- values: bfloat16 [16384, 6, 128], P(('dp', 'ctx'), 'mp'), parts along dimension 0, may hold values from -6 to 6
Outputs:
- hyena_out: bfloat16 [16384, 4608], P(('dp', 'ctx'), 'mp'), parts along dimension 0
- attn_out: bfloat16 [16384, 48, 128], P(('dp', 'ctx'), 'mp'), parts along dimension 0
There are 4 independent parts, one for each index of `dp`. A program takes and returns all parts, laid end to end along the dimension named above; an argument that names none is the same for every part. Nothing has to cross between parts.
All inputs are finite; a program needn't handle non-finite values.
Results may differ from a plain program's by a relative error of at most 0.01.
Values may be sent and summed in bfloat16 or wider, within the bound.
No kernel may reach another device: no remote copies, remote signals or barrier semaphores. Data moves between devices by JAX's collectives and lax.ppermute only.
A program may use at most 64 MiB of HBM per device.

v0:
```python
import math

import jax
import jax.numpy as jnp
from jax import lax
from jax.sharding import PartitionSpec as P

GSIZE = 16


def shifted(value, axis, steps):
    count = lax.axis_size(axis)
    initial, last = (max(0, -steps), min(count, count - steps))
    return lax.ppermute(value, axis, [(source, source + steps) for source in range(initial, last)])


def body(streams, short_taps, modal_residue, modal_rate, skip_gain, queries, keys, values):
    tok_rows = streams.shape[0]
    reach = short_taps.shape[0] - 1
    groups_dev = modal_rate.shape[1]
    rim = shifted(streams[tok_rows - reach :], "ctx", 1)
    extended = jnp.concatenate([rim, streams], axis=0).astype(jnp.float32)
    taps_full = jnp.repeat(short_taps, GSIZE, axis=2)
    filtered = jnp.zeros(streams.shape, jnp.float32)
    for offset in range(reach + 1):
        filtered = (
            filtered + taps_full[offset] * extended[reach - offset : reach - offset + tok_rows]
        )
    gated = (filtered[:, 1] * filtered[:, 2]).astype(jnp.bfloat16)
    gated_float = gated.astype(jnp.float32).reshape(tok_rows, groups_dev, GSIZE)
    anchor = lax.axis_index("ctx") * tok_rows
    anchor_float = anchor.astype(jnp.float32)
    highest = lax.Precision.HIGHEST
    piece = lax.all_gather(gated, "ctx", axis=0, tiled=True)
    count = piece.shape[0]
    lag = anchor_float - jnp.arange(count, dtype=jnp.int32).astype(jnp.float32)
    decay = jnp.exp(-modal_rate[:, :, None] * jnp.maximum(lag, 0.0)[None, None, :])
    decay = jnp.where(lag[None, None, :] > 0.0, decay, 0.0)
    source = piece.astype(jnp.float32).reshape(count, groups_dev, GSIZE)
    state = jnp.einsum("ngs,sgc->ngc", decay, source, precision=highest)
    positions = jnp.arange(tok_rows, dtype=jnp.int32)
    coeff = modal_residue[:, :, None] * jnp.exp(
        -modal_rate[:, :, None] * positions.astype(jnp.float32)[None, None, :]
    )
    far_term = jnp.einsum("ngt,ngc->tgc", coeff, state, precision=highest)
    table = jnp.sum(coeff, axis=0)
    offsets = positions[:, None] - positions[None, :]
    toeplitz = jnp.where(offsets[None] >= 0, jnp.take(table, jnp.maximum(offsets, 0), axis=1), 0.0)
    near_term = jnp.einsum("gts,sgc->tgc", toeplitz, gated_float, precision=highest)
    long_term = (far_term + near_term).reshape(tok_rows, -1)
    hyena_out = (filtered[:, 0] * (long_term + skip_gain * gated.astype(jnp.float32))).astype(
        jnp.bfloat16
    )
    heads_dev = queries.shape[1]
    head_size = queries.shape[2]
    scale = 1.0 / math.sqrt(head_size)
    target = anchor + positions
    last_target = anchor + tok_rows - 1
    start_state = (
        jnp.full((heads_dev, tok_rows), -1e30, jnp.float32),
        jnp.zeros((heads_dev, tok_rows), jnp.float32),
        jnp.zeros((heads_dev, tok_rows, head_size), jnp.float32),
    )
    piece = (
        lax.all_gather(keys, "ctx", axis=0, tiled=True),
        lax.all_gather(values, "ctx", axis=0, tiled=True),
    )
    key_rows = piece[0][:, 0]
    value_rows = piece[1][:, 0]
    count = key_rows.shape[0]
    span = 512

    def visit(number, inner):
        begin = number * span

        def update(state_in):
            largest, total, accum = state_in
            key_block = lax.dynamic_slice_in_dim(key_rows, begin, span, 0)
            value_block = lax.dynamic_slice_in_dim(value_rows, begin, span, 0)
            source = begin + jnp.arange(span, dtype=jnp.int32)
            scores = (
                jnp.einsum("thd,sd->hts", queries, key_block, preferred_element_type=jnp.float32)
                * scale
            )
            visible = source[None, None, :] <= target[None, :, None]
            masked = jnp.where(visible, scores, -1e30)
            renewed = jnp.maximum(largest, jnp.max(masked, axis=-1))
            correction = jnp.exp(largest - renewed)
            weights = jnp.where(visible, jnp.exp(scores - renewed[..., None]), 0.0)
            total = total * correction + jnp.sum(weights, axis=-1)
            mixed = jnp.einsum(
                "hts,sd->htd",
                weights.astype(jnp.bfloat16),
                value_block,
                preferred_element_type=jnp.float32,
            )
            accum = accum * correction[..., None] + mixed
            return (renewed, total, accum)

        def unchanged(state_in):
            return state_in

        return lax.cond(begin <= last_target, update, unchanged, inner)

    largest, total, accum = lax.fori_loop(0, count // span, visit, start_state)
    attn_out = jnp.transpose(accum / total[..., None], (1, 0, 2)).astype(jnp.bfloat16)
    return (hyena_out, attn_out)


def solution(mesh):
    in_specs = (
        P(("dp", "ctx"), None, "mp"),
        P(None, None, "mp"),
        P(None, "mp"),
        P(None, "mp"),
        P("mp"),
        P(("dp", "ctx"), "mp", None),
        P(("dp", "ctx"), "mp", None),
        P(("dp", "ctx"), "mp", None),
    )
    out_specs = (P(("dp", "ctx"), "mp"), P(("dp", "ctx"), "mp", None))
    return jax.shard_map(body, mesh=mesh, in_specs=in_specs, out_specs=out_specs, check_vma=False)
```

profile of v0, /device:TPU:6, one launch (start us, length us, event | category | flops | bytes accessed | tf_op | source)
XLA Modules:
  0.0 389.2 jit_solution(10997604427805677534)
XLA Ops:
  7.2 0.7 all-gather.5.cloned.1.call-update
  7.9 0.7 all-gather.7.cloned.1.call-update
  8.7 0.8 slice.84
  9.5 3.5 collective-permute-start
  13.0 1.0 fusion.66
  14.0 1.4 copy.31
  16.7 0.3 copy.30
  17.0 0.5 maximum_convert_fusion
  17.5 4.4 %fusion.43 = f32[128,3,768]{0,2,1:T(8,128)S(1)} fusion(f32[134,3,768]{0,2,1:T(8,128)S(1)} %maximum_convert_fusion, f32[3,768]{1,0:T(4,128)S(1)} %broadcast_in_dim.118, f32[3,768]{1,0:T(4,128)S(1)} %broadcast_in_dim.116, f32[3,768]{1,0:T(4,128)S(1)} %broadcast_in_dim.114, f32[3,768]{1,0:T(4,128)S(1)} %broadcast_in_dim.112, ...), kind=kLoop, calls=%fused_computation.47 | loop fusion | flops 3833856 | bytes 9501696 | tf_op jit(solution)/shard_map/add | solution.py:27
  22.0 1.0 copy-done
  23.0 0.7 fusion.50
  24.0 0.3 fusion.54
  24.4 54.8 %gather_fusion = f32[16384,48]{1,0:T(8,128)} fusion(f32[48,128]{0,1:T(8,128)S(1)} %copy.35, s32[16384]{0:T(1024)S(1)} %bitcast_clamp_fusion), kind=kCustom, calls=%fused_computation | custom fusion | bytes 6356992 | tf_op jit(solution)/shard_map/jit(_take)/gather | solution.py:48
  79.2 5.8 %copy.36 = f32[128,128,48]{1,0,2:T(8,128)S(1)} copy(f32[128,128,48]{2,1,0:T(8,128)} %bitcast.70) | data formatting | bytes 6291456 | tf_op jit(solution)/shard_map/jit(_take)/gather | solution.py:48
  85.0 1.0 copy.37
  86.1 26.1 %all-gather.5.cloned.1.call-done = bf16[4096,1,128]{2,0,1:T(8,128)(2,1)} async-done(((bf16[128,1,128]{2,0,1:T(8,128)(2,1)}), bf16[4096,1,128]{2,0,1:T(8,128)(2,1)}) %all-gather.5.cloned.1.call-update) | async-done | bytes 1048592 | tf_op jit(solution)/shard_map/all_gather | solution.py:65
  112.2 92.2 %all-gather.7.cloned.1.call-done = bf16[4096,1,128]{2,0,1:T(8,128)(2,1)} async-done(((bf16[128,1,128]{2,0,1:T(8,128)(2,1)}), bf16[4096,1,128]{2,0,1:T(8,128)(2,1)}) %all-gather.7.cloned.1.call-update) | async-done | bytes 1048592 | tf_op jit(solution)/shard_map/all_gather | solution.py:66
  204.4 0.8 broadcast_in_dim.127
  205.2 4.9 %while.18 = (s32[]{:T(128)}, f32[8,128]{1,0:T(8,128)S(1)}, f32[8,128]{1,0:T(8,128)S(1)}, f32[8,128,128]{2,1,0:T(8,128)}, s32[]{:T(128)}, /*index=5*/bf16[4096,12...) while((s32[]{:T(128)}, f32[8,128]{1,0:T(8,128)S(1)}, ...), condition=%wide.region_6.7_spmd.clone, body=%wide.region_1.6_spmd.clone.sunk | while | flops 274532992 | bytes 12392817 | solution.py:105
  205.2 4.6 %conditional.3 = ((f32[8,128]{1,0:T(8,128)S(1)}, f32[8,128]{1,0:T(8,128)S(1)}, f32[8,128,128]{2,1,0:T(8,128)})) conditional(s32[]{:T(128)} %convert_element_type.87, (f32[8,128]{1,0:T(8,128)S(1)}, f32[8,128]{1,0:T(8,128)S(1)}, f32[8,128,128]{2,1,0:T(8,128)}) %tuple.63, (s32[]{:T(128)}, s32[]{:T(128)}, bf16[4096,128]{1,0:T(8,128)(2,1)}, ...), branch_computations={%region_2.2_spmd, %region_3.5_spmd} | conditional | flops 274532992 | bytes 12392074 | solution.py:103
  205.2 0.1 broadcast_compare_fusion
  205.4 1.4 fusion.2
  206.8 0.4 fusion.6
  207.3 1.7 convolution_add_fusion
  209.0 0.8 copy-done.3
  210.2 2.1 fusion.56
  212.3 154.0 %all-gather.9.cloned.1.call-done = bf16[4096,1,768]{0,2,1:T(8,128)(2,1)} async-done(((bf16[128,1,768]{0,2,1:T(8,128)(2,1)}), bf16[4096,1,768]{0,2,1:T(8,128)(2,1)}) %all-gather.9.cloned.1.call-update) | async-done | bytes 6291472 | tf_op jit(solution)/shard_map/all_gather | solution.py:34
  366.2 12.1 %fusion.40 = f32[16,48,16]{0,2,1:T(8,128)S(1)} fusion(bf16[4096,48,16]{0,2,1:T(8,128)(2,1)} %bitcast.74, f32[4096]{0:T(1024)S(1)} %fusion.61, f32[16,48]{0,1:T(8,128)S(1)} %copy.32, pred[4096]{0:T(1024)(128)(4,1)S(1)} %fusion.62), kind=kOutput, calls=%fused_computation.45 | convolution fusion | flops 610271232 | bytes 6364160 | tf_op jit(solution)/shard_map/ngs,sgc->ngc/dot_general | solution.py:40
  378.3 0.7 fusion.55
  379.0 2.6 fusion.37
  381.6 0.2 fusion.52
  381.8 0.8 copy.40
  (69 shorter events, 2.0 us)
Async XLA Ops:
  7.2 105.0 %all-gather.5.cloned.1.call-start = ((), (), s32[]{:S(2)}) async-start(), calls=%async_computation | async-start | bytes 1081344 | tf_op jit(solution)/shard_map/all_gather | solution.py:65
  7.9 196.5 %all-gather.7.cloned.1.call-start = ((), (), s32[]{:S(2)}) async-start(), calls=%async_computation.1 | async-start | bytes 1081344 | tf_op jit(solution)/shard_map/all_gather | solution.py:66
  8.6 357.6 %all-gather.9.cloned.1.call-start = ((), (), s32[]{:S(2)}) async-start(), calls=%async_computation.2 | async-start | bytes 6488064 | tf_op jit(solution)/shard_map/all_gather | solution.py:34
  9.5 7.2 %collective-permute-start = (bf16[6,3,768]{2,0,1:T(8,128)(2,1)S(1)}, bf16[6,3,768]{2,0,1:T(8,128)(2,1)S(1)}, u32[]{:S(2)}, u32[]{:S(2)}) collective-permute-start(bf16[6,3,768]{2,0,1:T(8,128)(2,1)S(1)} %slice.84), channel_id=1, source_target_pairs={{0,6},{6,12},{12,18},{18,24},{24,30},{30,36},{36,42},{42,48},{48,5... | collective-permute-start | bytes 82952 | tf_op jit(solution)/shard_map/ppermute | solution.py:14
  17.5 6.3 %copy-start.5 = (f32[16,48]{1,0:T(8,128)S(1)}, f32[16,48]{1,0:T(8,128)}, u32[]{:S(2)}) copy-start(f32[16,48]{1,0:T(8,128)} %param.15) | copy-start | bytes 9220
  17.5 6.3 %copy-start.6 = (f32[16,48]{1,0:T(8,128)S(1)}, f32[16,48]{1,0:T(8,128)}, u32[]{:S(2)}) copy-start(f32[16,48]{1,0:T(8,128)} %param.14) | copy-start | bytes 9220
  22.0 1.1 copy-start
  205.4 1.9 copy-start.2
  209.0 0.8 copy-start.3
  366.2 12.8 %copy-start.4 = (bf16[128,1,768]{0,2,1:T(8,128)(2,1)S(1)}, bf16[128,1,768]{0,2,1:T(8,128)(2,1)}, u32[]{:S(2)}) copy-start(bf16[128,1,768]{0,2,1:T(8,128)(2,1)} %fusion.50) | copy-start | bytes 589828
  379.0 2.6 copy-start.1
  379.0 2.6 copy-start.7
Sparse Core Ops, SparseCore 0:
  11.8 100.3 all-gather.4
  115.9 88.4 all-gather.6
  208.6 157.6 all-gather.8
where the time goes:
time: 392 us; the launch traced here: 389 us
  waiting for transfers between devices  274 us (70%)
  local copies, waits for them, and re-layouts  70.3 us (18%)
  matrix products  18.4 us (5%)
  between operations  14 us (4%)
  other arithmetic  8.84 us (2%)
    all_gather x1, waiting for transfers between devices, body(): piece = lax.all_gather(gated, 'ctx', axis=0, tiled=True)  154 us
    all_gather x1, waiting for transfers between devices, body(): lax.all_gather(values, 'ctx', axis=0, tiled=True)  92.2 us
    gather x2, local copies, waits for them, and re-layouts, body(): jnp.take(table, jnp.maximum(offsets, 0), axis=1)  60.6 us
    all_gather x1, waiting for transfers between devices, body(): lax.all_gather(keys, 'ctx', axis=0, tiled=True)  26.1 us
    dot_general x1, matrix products, body(): state = jnp.einsum('ngs,sgc->ngc', decay, source, precision=highest)  12.1 us
  transfers between devices with their start and end apart: 4, of which 3 were waited for; matrix products, arithmetic and copies ran while one was open for 20% of the time, Pallas kernels for 0%

commit v1 on v0

v1 whole, which is shorter than its diff:
```python
import functools
import math

import jax
import jax.numpy as jnp
from jax import lax
from jax.experimental import pallas as pl
from jax.experimental.pallas import tpu as pltpu
from jax.sharding import Mesh, PartitionSpec as P

GSIZE = 16
LANES = 128
LOG2E = 1.4426950408889634
HIGHEST = lax.Precision.HIGHEST
F32 = jnp.float32
BF16 = jnp.bfloat16


def vmem(count):
    return [pl.BlockSpec(memory_space=pltpu.VMEM)] * count


def smem():
    return pl.BlockSpec(memory_space=pltpu.SMEM)


def call(kernel, out_shape, in_specs, flops, moved, scratch=()):
    many = isinstance(out_shape, (list, tuple))
    return pl.pallas_call(
        kernel,
        out_shape=out_shape,
        in_specs=in_specs,
        out_specs=vmem(len(out_shape)) if many else vmem(1)[0],
        scratch_shapes=list(scratch),
        compiler_params=pltpu.CompilerParams(vmem_limit_bytes=32 * 1024 * 1024),
        cost_estimate=pl.CostEstimate(flops=flops, bytes_accessed=moved, transcendentals=0),
    )


def iota(shape, dim):
    return lax.broadcasted_iota(jnp.int32, shape, dim)


def split(value):
    high = value.astype(BF16)
    return high, (value - high.astype(F32)).astype(BF16)


def filter_kernel(st_ref, rim_ref, taps_ref, rate_ref, first_ref, gated_ref, state_ref, ext):
    rows, width = gated_ref.shape
    pad = rim_ref.shape[1]
    taps = taps_ref.shape[0] // 3
    row = iota((rows, LANES), 0).astype(F32)
    same = iota((LANES, LANES), 0) // GSIZE == iota((LANES, LANES), 1) // GSIZE
    for tile in range(width // LANES):
        cols = slice(tile * LANES, (tile + 1) * LANES)
        for j in range(3):
            ext[j, :pad, :] = rim_ref[j, :, cols].astype(F32)
            ext[j, pad:, :] = st_ref[j, :, cols].astype(F32)
        filtered = []
        for j in range(3):
            total = taps_ref[j : j + 1, cols] * ext[j, pad : pad + rows, :]
            for k in range(1, taps):
                tap = taps_ref[3 * k + j : 3 * k + j + 1, cols]
                total = total + tap * ext[j, pad - k : pad - k + rows, :]
            filtered.append(total)
        first_ref[:, cols] = filtered[0]
        gated = (filtered[1] * filtered[2]).astype(BF16)
        gated_ref[:, cols] = gated
        decay = jnp.exp(-rate_ref[:, cols] * (float(rows) - row)).T
        high, low = split(decay)
        full = jnp.dot(high, gated, preferred_element_type=F32) + jnp.dot(
            low, gated, preferred_element_type=F32
        )
        full = jnp.where(same, full, 0.0)
        state = full[:GSIZE]
        for g in range(1, LANES // GSIZE):
            state = state + full[g * GSIZE : (g + 1) * GSIZE]
        state_ref[:, cols] = state


def near_kernel(gated_ref, rate_ref, res_ref, near_ref):
    rows, width = gated_ref.shape
    per = LANES // GSIZE
    row = iota((rows, LANES), 0).astype(F32)
    group = iota((rows, LANES), 1) // GSIZE
    causal = iota((rows, LANES), 0) >= iota((rows, LANES), 1)
    for tile in range(width // LANES):
        cols = slice(tile * LANES, (tile + 1) * LANES)
        rate = rate_ref[:, cols]
        coeff = res_ref[:, cols] * jnp.exp(-rate * row)
        grow = jnp.exp(rate * row).T
        gated = gated_ref[:, cols]
        grow_high, grow_low = split(grow)
        coeff_high, coeff_low = split(coeff)
        zero = jnp.zeros_like(coeff_high)
        stack_high = jnp.concatenate([jnp.where(group == g, coeff_high, zero) for g in range(per)], 0)
        stack_low = jnp.concatenate([jnp.where(group == g, coeff_low, zero) for g in range(per)], 0)
        table = (
            jnp.dot(stack_high, grow_high, preferred_element_type=F32)
            + jnp.dot(stack_high, grow_low, preferred_element_type=F32)
            + jnp.dot(stack_low, grow_high, preferred_element_type=F32)
        )
        table = jnp.where(jnp.concatenate([causal] * per, 0), table, 0.0).astype(BF16)
        every = jnp.dot(table, gated, preferred_element_type=F32)
        near = jnp.zeros((rows, LANES), F32)
        for g in range(per):
            near = jnp.where(group == g, every[g * rows : (g + 1) * rows], near)
        near_ref[:, cols] = near


def join_kernel(first_ref, gated_ref, near_ref, past_ref, rate_ref, res_ref, gain_ref, out_ref):
    rows, width = gated_ref.shape
    row = iota((rows, LANES), 0).astype(F32)
    same = iota((LANES, LANES), 0) // GSIZE == iota((LANES, LANES), 1) // GSIZE
    for tile in range(width // LANES):
        cols = slice(tile * LANES, (tile + 1) * LANES)
        coeff_high, coeff_low = split(res_ref[:, cols] * jnp.exp(-rate_ref[:, cols] * row))
        past = jnp.concatenate([past_ref[:, cols]] * (LANES // GSIZE), 0)
        past_high, past_low = split(jnp.where(same, past, 0.0))
        far = (
            jnp.dot(coeff_high, past_high, preferred_element_type=F32)
            + jnp.dot(coeff_high, past_low, preferred_element_type=F32)
            + jnp.dot(coeff_low, past_high, preferred_element_type=F32)
        )
        direct = gain_ref[:, cols] * gated_ref[:, cols].astype(F32)
        out_ref[:, cols] = (first_ref[:, cols] * (far + near_ref[:, cols] + direct)).astype(BF16)


def attend_kernel(first, last, rows, scale, where_ref, q_ref, kv_ref, *refs):
    blocks = kv_ref.shape[0] // rows
    heads = q_ref.shape[0] // rows
    if first:
        acc_out, ml_out = refs
    elif last:
        acc_in, ml_in, out_ref = refs
    else:
        acc_in, ml_in, acc_out, ml_out = refs
    chunk = 256
    keys = kv_ref[:, :LANES]
    values = jnp.concatenate([kv_ref[:, LANES:], jnp.ones((kv_ref.shape[0], LANES), BF16)], 1)
    lane_block = iota((1, kv_ref.shape[0]), 1) // rows
    bias = jnp.zeros((1, kv_ref.shape[0]), F32)
    for b in range(1 if first else 0, blocks):
        bias = bias + jnp.where((lane_block == b) & (where_ref[b] == 0), -1e30, 0.0)

    for number in range(q_ref.shape[0] // chunk):
        span = slice(number * chunk, (number + 1) * chunk)
        scores = lax.dot_general(
            q_ref[span, :], keys, (((1,), (1,)), ((), ())), preferred_element_type=F32
        )
        scores = scores * scale + bias
        if first:
            target = (number * chunk + iota(scores.shape, 0)) // heads
            source = iota(scores.shape, 1)
            scores = jnp.where((source > target) & (source < rows), -1e30, scores)
        largest = jnp.max(scores, axis=1, keepdims=True)
        if not first:
            before = ml_in[span, :1]
            largest = jnp.maximum(largest, before)
        weights = jnp.exp2(scores - largest).astype(BF16)
        mixed = jnp.dot(weights, values, preferred_element_type=F32)
        total = mixed[:, LANES : 2 * LANES]
        mixed = mixed[:, :LANES]
        if not first:
            shrink = jnp.exp2(before - largest)
            mixed = mixed + acc_in[span, :] * shrink
            total = total + ml_in[span, LANES - 1 :] * shrink
        if last:
            out_ref[span, :] = (mixed / total).astype(BF16)
        else:
            acc_out[span, :] = mixed
            lane = iota((chunk, LANES), 1)
            ml_out[span, :] = jnp.where(lane < LANES // 2, largest, total)


def body(streams, short_taps, modal_residue, modal_rate, skip_gain, queries, keys, values):
    rows, kinds, width = streams.shape
    taps = short_taps.shape[0]
    modes, groups = modal_rate.shape
    heads, size = queries.shape[1:]
    layers, ring, parts = lax.axis_size("zh"), lax.axis_size("y"), lax.axis_size("mp")
    layer, place = lax.axis_index("zh"), lax.axis_index("y")
    side = lax.axis_index("mp") % 2
    devices = layers * ring

    kv = jnp.concatenate([keys[:, 0], values[:, 0]], axis=1)
    held = [kv] + [
        lax.ppermute(kv, "zh", [(z, z + s) for z in range(layers - s)]) for s in range(1, layers)
    ]
    held = jnp.concatenate(held, axis=0)

    by_kind = jnp.transpose(streams, (1, 0, 2))
    rim = lax.ppermute(by_kind[:, rows - 8 :], ("zh", "y"), [(i, i + 1) for i in range(devices - 1)])
    taps_full = jnp.repeat(short_taps.reshape(taps * kinds, groups), GSIZE, axis=1)
    rate_full = jnp.repeat(modal_rate, GSIZE, axis=1)
    rate_row = modal_rate.T.reshape(1, groups * modes)
    res_row = modal_residue.T.reshape(1, groups * modes)
    wide = jax.ShapeDtypeStruct((rows, width), F32)
    first, gated, state = call(
        filter_kernel,
        [wide, jax.ShapeDtypeStruct((rows, width), BF16), jax.ShapeDtypeStruct((modes, width), F32)],
        vmem(4),
        4_000_000_000,
        4_000_000,
        [pltpu.VMEM((3, rows + 8, LANES), F32)],
    )(by_kind, rim, taps_full, rate_row)
    near = call(near_kernel, wide, vmem(3), 4_000_000_000, 4_000_000)(gated, rate_row, res_row)

    past = jnp.zeros_like(state)
    step_rate = -rate_full * float(rows)
    step = 1
    while step < devices:
        full = state + jnp.exp(step_rate) * past
        come = lax.ppermute(full, ("zh", "y"), [(i, i + step) for i in range(devices - step)])
        past = past + jnp.exp(step_rate * (step - 1.0)) * come
        step *= 2
    hyena_out = call(
        join_kernel,
        jax.ShapeDtypeStruct((rows, width), BF16),
        vmem(7),
        500_000_000,
        2_000_000,
    )(first, gated, near, past, rate_row, res_row, skip_gain.reshape(1, width))

    rows_q = queries.reshape(rows * heads, size)
    scale = LOG2E / math.sqrt(size)
    pairs = [
        (y * parts + m, ((y + (1 if m % 2 == 0 else -1)) % ring) * parts + m)
        for y in range(ring)
        for m in range(parts)
    ]
    state_shape = [jax.ShapeDtypeStruct((rows * heads, LANES), F32)] * 2
    carry = ()
    attn_out = None
    for step in range(ring):
        origin = (place + jnp.where(side == 0, -step, step)) % ring
        visible = jnp.concatenate(
            [(origin < place)[None], layer >= jnp.arange(1, layers)]
        ).astype(jnp.int32)
        last = step == ring - 1
        carry = call(
            functools.partial(attend_kernel, step == 0, last, rows, scale),
            jax.ShapeDtypeStruct((rows * heads, size), BF16) if last else state_shape,
            [smem()] + vmem(2 + len(carry)),
            1_000_000_000,
            3_000_000,
        )(visible, rows_q, held, *carry)
        if not last:
            held = lax.ppermute(held, ("y", "mp"), pairs)
    attn_out = carry.reshape(rows, heads, size)
    return hyena_out, attn_out


def solution(mesh):
    names = ("dp", "zh", "y", "mp")
    dp, ctx, mp = (mesh.shape[name] for name in ("dp", "ctx", "mp"))
    ring = 8 if ctx % 8 == 0 else ctx
    finer = Mesh(mesh.devices.reshape(dp, ctx // ring, ring, mp), names)
    pos = ("dp", "zh", "y")
    in_specs = (
        P(pos, None, "mp"),
        P(None, None, "mp"),
        P(None, "mp"),
        P(None, "mp"),
        P("mp"),
        P(pos, "mp", None),
        P(pos, "mp", None),
        P(pos, "mp", None),
    )
    out_specs = (P(pos, "mp"), P(pos, "mp", None))
    return jax.shard_map(body, mesh=finer, in_specs=in_specs, out_specs=out_specs, check_vma=False)
```

time: 392 us -> 129 us (0.33)
  the two profiles are of different devices: /device:TPU:6 before, /device:TPU:178 now
where the time goes in v1:
time: 129 us; the launch traced here: 128 us
  starting transfers between devices  85 us (66%)
  Pallas kernels  26 us (20%)
  waiting for transfers between devices  10 us (8%)
  local copies, waits for them, and re-layouts  5.07 us (4%)
    ppermute x7, starting transfers between devices, body(): held = lax.ppermute(held, ('y', 'mp'), pairs)  39.6 us
    ppermute x5, starting transfers between devices, body(): lax.ppermute(full, ('zh', 'y'), [(i, i + step) for i in range(devices - s...  23.6 us
    pallas_call x8, Pallas kernels, body(): call(functools.partial(attend_kernel, step == 0, last, rows, scale), jax....  20.5 us
    ppermute x3, starting transfers between devices, body(): lax.ppermute(kv, 'zh', [(z, z + s) for z in range(layers - s)])  19.2 us
    ppermute x7, waiting for transfers between devices, body(): held = lax.ppermute(held, ('y', 'mp'), pairs)  5.47 us
    ppermute x5, waiting for transfers between devices, body(): lax.ppermute(full, ('zh', 'y'), [(i, i + step) for i in range(devices - s...  3.43 us
    pallas_call x1, Pallas kernels, body(): call(near_kernel, wide, vmem(3), 4000000000, 4000000)  3.39 us
  transfers between devices with their start and end apart: 16, of which 5 were waited for; matrix products, arithmetic and copies ran while one was open for 3% of the time, Pallas kernels for 18%

profile of v1, /device:TPU:178, one launch (start us, length us, event | category | flops | bytes accessed | tf_op | source)
XLA Modules:
  0.0 128.4 jit_solution(3631449667955402066)
XLA Ops:
  1.4 9.1 %collective-permute-start.6 = (bf16[128,256]{1,0:T(8,128)(2,1)S(1)}, bf16[128,256]{1,0:T(8,128)(2,1)S(1)}, u32[]{:S(2)}, u32[]{:S(2)}) collective-permute-start(bf16[128,256]{1,0:T(8,128)(2,1)S(1)} %pad_maximum_fusion.1), channel_id=1, source_target_pairs={{0,48},{48,96},{96,144},{1,49},{49,97},{97,145},{2,50},{50,98},{98... | collective-permute-start | bytes 196616 | tf_op jit(solution)/shard_map/ppermute | solution.py:189
  10.5 8.8 %collective-permute-start.7 = (bf16[128,256]{1,0:T(8,128)(2,1)S(1)}, bf16[128,256]{1,0:T(8,128)(2,1)S(1)}, u32[]{:S(2)}, u32[]{:S(2)}) collective-permute-start(bf16[128,256]{1,0:T(8,128)(2,1)S(1)} %pad_maximum_fusion.1), channel_id=1, source_target_pairs={{0,96},{48,144},{1,97},{49,145},{2,98},{50,146},{3,99},{51,147},{4... | collective-permute-start | bytes 196616 | tf_op jit(solution)/shard_map/ppermute | solution.py:189
  19.4 1.3 %collective-permute-start.8 = (bf16[128,256]{1,0:T(8,128)(2,1)S(1)}, bf16[128,256]{1,0:T(8,128)(2,1)S(1)}, u32[]{:S(2)}, u32[]{:S(2)}) collective-permute-start(bf16[128,256]{1,0:T(8,128)(2,1)S(1)} %pad_maximum_fusion.1), channel_id=1, source_target_pairs={{0,144},{1,145},{2,146},{3,147},{4,148},{5,149},{6,150},{7,151},{8... | collective-permute-start | bytes 196616 | tf_op jit(solution)/shard_map/ppermute | solution.py:189
  21.5 2.6 %collective-permute-start = (bf16[3,8,768]{2,1,0:T(8,128)(2,1)S(1)}, bf16[3,8,768]{2,1,0:T(8,128)(2,1)S(1)}, u32[]{:S(2)}, u32[]{:S(2)}) collective-permute-start(bf16[3,8,768]{2,1,0:T(8,128)(2,1)S(1)} %slice.4), channel_id=1, source_target_pairs={{0,6},{6,12},{12,18},{18,24},{24,30},{30,36},{36,42},{42,48},{48,5... | collective-permute-start | bytes 110600 | tf_op jit(solution)/shard_map/ppermute | solution.py:194
  26.2 1.1 collective-permute-done.rim_ref
  27.3 1.0 shard_map.95
  28.4 2.6 %collective-permute-start.1 = (f32[16,768]{1,0:T(8,128)S(1)}, f32[16,768]{1,0:T(8,128)S(1)}, u32[]{:S(2)}, u32[]{:S(2)}) collective-permute-start(f32[16,768]{1,0:T(8,128)S(1)} %multiply_add_fusion.8), channel_id=1, source_target_pairs={{0,6},{6,12},{12,18},{18,24},{24,30},{30,36},{36,42},{42,48},{48,5... | collective-permute-start | bytes 147464 | tf_op jit(solution)/shard_map/ppermute | solution.py:215
  31.1 7.2 %collective-permute-start.9 = (bf16[512,256]{1,0:T(8,128)(2,1)S(1)}, bf16[512,256]{1,0:T(8,128)(2,1)S(1)}, u32[]{:S(2)}, u32[]{:S(2)}) collective-permute-start(bf16[512,256]{1,0:T(8,128)(2,1)S(1)} %pad_maximum_fusion.kv_ref), channel_id=1, source_target_pairs={{0,6},{1,43},{2,8},{3,45},{4,10},{5,47},{6,12},{7,1},{8,14},{9,3},... | collective-permute-start | bytes 786440 | tf_op jit(solution)/shard_map/ppermute | solution.py:250
  38.3 9.4 %collective-permute-start.2 = (f32[16,768]{1,0:T(8,128)S(1)}, f32[16,768]{1,0:T(8,128)S(1)}, u32[]{:S(2)}, u32[]{:S(2)}) collective-permute-start(f32[16,768]{1,0:T(8,128)S(1)} %get-tuple-element.38), channel_id=1, source_target_pairs={{0,12},{6,18},{12,24},{18,30},{24,36},{30,42},{36,48},{42,54},{48,... | collective-permute-start | bytes 147464 | tf_op jit(solution)/shard_map/ppermute | solution.py:215
  47.8 2.1 %collective-permute-done.2 = f32[16,768]{1,0:T(8,128)S(1)} collective-permute-done((f32[16,768]{1,0:T(8,128)S(1)}, f32[16,768]{1,0:T(8,128)S(1)}, u32[]{:S(2)}, u32[]{:S(2)}) %collective-permute-start.2) | collective-permute-done | bytes 49184 | tf_op jit(solution)/shard_map/ppermute | solution.py:215
  50.0 4.2 %collective-permute-start.3 = (f32[16,768]{1,0:T(8,128)S(1)}, f32[16,768]{1,0:T(8,128)S(1)}, u32[]{:S(2)}, u32[]{:S(2)}) collective-permute-start(f32[16,768]{1,0:T(8,128)S(1)} %multiply_add_fusion.5), channel_id=1, source_target_pairs={{0,24},{6,30},{12,36},{18,42},{24,48},{30,54},{36,60},{42,66},{48,... | collective-permute-start | bytes 147464 | tf_op jit(solution)/shard_map/ppermute | solution.py:215
  54.2 1.9 %collective-permute-start.10 = (bf16[512,256]{1,0:T(8,128)(2,1)S(1)}, bf16[512,256]{1,0:T(8,128)(2,1)S(1)}, u32[]{:S(2)}, u32[]{:S(2)}) collective-permute-start(bf16[512,256]{1,0:T(8,128)(2,1)S(1)} %collective-permute-done.9.kv_ref), channel_id=1, source_target_pairs={{0,6},{1,43},{2,8},{3,45},{4,10},{5,47},{6,12},{7,1},{8,14},{9,3},... | collective-permute-start | bytes 786440 | tf_op jit(solution)/shard_map/ppermute | solution.py:250
  58.6 1.3 %collective-permute-done.3 = f32[16,768]{1,0:T(8,128)S(1)} collective-permute-done((f32[16,768]{1,0:T(8,128)S(1)}, f32[16,768]{1,0:T(8,128)S(1)}, u32[]{:S(2)}, u32[]{:S(2)}) %collective-permute-start.3) | collective-permute-done | bytes 49184 | tf_op jit(solution)/shard_map/ppermute | solution.py:215
  59.9 4.9 %collective-permute-start.4 = (f32[16,768]{1,0:T(8,128)S(1)}, f32[16,768]{1,0:T(8,128)S(1)}, u32[]{:S(2)}, u32[]{:S(2)}) collective-permute-start(f32[16,768]{1,0:T(8,128)S(1)} %get-tuple-element.36), channel_id=1, source_target_pairs={{0,48},{6,54},{12,60},{18,66},{24,72},{30,78},{36,84},{42,90},{48,... | collective-permute-start | bytes 147464 | tf_op jit(solution)/shard_map/ppermute | solution.py:215
  64.8 4.9 %collective-permute-start.11 = (bf16[512,256]{1,0:T(8,128)(2,1)S(1)}, bf16[512,256]{1,0:T(8,128)(2,1)S(1)}, u32[]{:S(2)}, u32[]{:S(2)}) collective-permute-start(bf16[512,256]{1,0:T(8,128)(2,1)S(1)} %collective-permute-done.10.kv_ref), channel_id=1, source_target_pairs={{0,6},{1,43},{2,8},{3,45},{4,10},{5,47},{6,12},{7,1},{8,14},{9,3},... | collective-permute-start | bytes 786440 | tf_op jit(solution)/shard_map/ppermute | solution.py:250
  69.7 3.4 %shard_map.96.near_ref = f32[128,768]{1,0:T(8,128)S(1)} custom-call(bf16[128,768]{1,0:T(8,128)(2,1)S(1)} %get-tuple-element.20.gated_ref, f32[1,768]{1,0:T(1,128)S(1)} %reshape.44.rate_ref, f32[1,768]{1,0:T(1,128)S(1)} %reshape.45.res_ref), custom_call_target="tpu_custom_call" | custom-call | flops 4000000000 | bytes 4000000 | tf_op jit(solution)/shard_map/pallas_call | solution.py:208
  73.1 2.7 %collective-permute-done.11.kv_ref = bf16[512,256]{1,0:T(8,128)(2,1)S(1)} collective-permute-done((bf16[512,256]{1,0:T(8,128)(2,1)S(1)}, bf16[512,256]{1,0:T(8,128)(2,1)S(1)}, u32[]{:S(2)}, u32[]{:S(2)}) %collective-permute-start.11) | collective-permute-done | bytes 262176 | tf_op jit(solution)/shard_map/ppermute | solution.py:250
  75.8 8.8 %collective-permute-start.12 = (bf16[512,256]{1,0:T(8,128)(2,1)S(1)}, bf16[512,256]{1,0:T(8,128)(2,1)S(1)}, u32[]{:S(2)}, u32[]{:S(2)}) collective-permute-start(bf16[512,256]{1,0:T(8,128)(2,1)S(1)} %collective-permute-done.11.kv_ref), channel_id=1, source_target_pairs={{0,6},{1,43},{2,8},{3,45},{4,10},{5,47},{6,12},{7,1},{8,14},{9,3},... | collective-permute-start | bytes 786440 | tf_op jit(solution)/shard_map/ppermute | solution.py:250
  84.6 2.4 %collective-permute-start.5 = (f32[16,768]{1,0:T(8,128)S(1)}, f32[16,768]{1,0:T(8,128)S(1)}, u32[]{:S(2)}, u32[]{:S(2)}) collective-permute-start(f32[16,768]{1,0:T(8,128)S(1)} %multiply_add_fusion.1), channel_id=1, source_target_pairs={{0,96},{6,102},{12,108},{18,114},{24,120},{30,126},{36,132},{42,13... | collective-permute-start | bytes 147464 | tf_op jit(solution)/shard_map/ppermute | solution.py:215
  87.1 1.5 %shard_map.98 = (f32[1024,128]{1,0:T(8,128)S(1)}, f32[1024,128]{1,0:T(8,128)S(1)}) custom-call(s32[4]{0:T(128)S(1)} %get-tuple-element.45.where_ref, bf16[1024,128]{1,0:T(8,128)(2,1)S(1)} %bitcast.17, bf16[512,256]{1,0:T(8,128)(2,1)S(1)} %pad_maximum_fusion.kv_ref), custom_call_target="tpu_custom_call" | custom-call | flops 1000000000 | bytes 3000000 | tf_op jit(solution)/shard_map/pallas_call | solution.py:242
  88.6 5.6 %collective-permute-start.13 = (bf16[512,256]{1,0:T(8,128)(2,1)S(1)}, bf16[512,256]{1,0:T(8,128)(2,1)S(1)}, u32[]{:S(2)}, u32[]{:S(2)}) collective-permute-start(bf16[512,256]{1,0:T(8,128)(2,1)S(1)} %collective-permute-done.12.kv_ref), channel_id=1, source_target_pairs={{0,6},{1,43},{2,8},{3,45},{4,10},{5,47},{6,12},{7,1},{8,14},{9,3},... | collective-permute-start | bytes 786440 | tf_op jit(solution)/shard_map/ppermute | solution.py:250
  94.3 1.0 shard_map.97
  95.3 2.8 %collective-permute-done.13.kv_ref = bf16[512,256]{1,0:T(8,128)(2,1)S(1)} collective-permute-done((bf16[512,256]{1,0:T(8,128)(2,1)S(1)}, bf16[512,256]{1,0:T(8,128)(2,1)S(1)}, u32[]{:S(2)}, u32[]{:S(2)}) %collective-permute-start.13) | collective-permute-done | bytes 262176 | tf_op jit(solution)/shard_map/ppermute | solution.py:250
  98.1 5.6 %collective-permute-start.14 = (bf16[512,256]{1,0:T(8,128)(2,1)S(1)}, bf16[512,256]{1,0:T(8,128)(2,1)S(1)}, u32[]{:S(2)}, u32[]{:S(2)}) collective-permute-start(bf16[512,256]{1,0:T(8,128)(2,1)S(1)} %collective-permute-done.13.kv_ref), channel_id=1, source_target_pairs={{0,6},{1,43},{2,8},{3,45},{4,10},{5,47},{6,12},{7,1},{8,14},{9,3},... | collective-permute-start | bytes 786440 | tf_op jit(solution)/shard_map/ppermute | solution.py:250
  103.7 2.6 %shard_map.99 = (f32[1024,128]{1,0:T(8,128)S(1)}, f32[1024,128]{1,0:T(8,128)S(1)}) custom-call(s32[4]{0:T(128)S(1)} %get-tuple-element.51.where_ref, bf16[1024,128]{1,0:T(8,128)(2,1)S(1)} %bitcast.18, bf16[512,256]{1,0:T(8,128)(2,1)S(1)} %collective-permute-done.9.kv_ref, f32[1024,128]{1,0:T(8,128)S(1)} %get-tuple-element.22.refs_0_, ...), custom_call_target="tpu_custom_call" | custom-call | flops 1000000000 | bytes 3000000 | tf_op jit(solution)/shard_map/pallas_call | solution.py:242
  106.3 2.6 %shard_map.100 = (f32[1024,128]{1,0:T(8,128)S(1)}, f32[1024,128]{1,0:T(8,128)S(1)}) custom-call(s32[4]{0:T(128)S(1)} %get-tuple-element.50.where_ref, bf16[1024,128]{1,0:T(8,128)(2,1)S(1)} %bitcast.19, bf16[512,256]{1,0:T(8,128)(2,1)S(1)} %collective-permute-done.10.kv_ref, f32[1024,128]{1,0:T(8,128)S(1)} %get-tuple-element.24.refs_0_, ...), custom_call_target="tpu_custom_call" | custom-call | flops 1000000000 | bytes 3000000 | tf_op jit(solution)/shard_map/pallas_call | solution.py:242
  109.0 2.6 %shard_map.101 = (f32[1024,128]{1,0:T(8,128)S(1)}, f32[1024,128]{1,0:T(8,128)S(1)}) custom-call(s32[4]{0:T(128)S(1)} %get-tuple-element.49.where_ref, bf16[1024,128]{1,0:T(8,128)(2,1)S(1)} %bitcast.20, bf16[512,256]{1,0:T(8,128)(2,1)S(1)} %collective-permute-done.11.kv_ref, f32[1024,128]{1,0:T(8,128)S(1)} %get-tuple-element.26.refs_0_, ...), custom_call_target="tpu_custom_call" | custom-call | flops 1000000000 | bytes 3000000 | tf_op jit(solution)/shard_map/pallas_call | solution.py:242
  111.6 5.6 %collective-permute-start.15 = (bf16[512,256]{1,0:T(8,128)(2,1)S(1)}, bf16[512,256]{1,0:T(8,128)(2,1)S(1)}, u32[]{:S(2)}, u32[]{:S(2)}) collective-permute-start(bf16[512,256]{1,0:T(8,128)(2,1)S(1)} %collective-permute-done.14.kv_ref), channel_id=1, source_target_pairs={{0,6},{1,43},{2,8},{3,45},{4,10},{5,47},{6,12},{7,1},{8,14},{9,3},... | collective-permute-start | bytes 786440 | tf_op jit(solution)/shard_map/ppermute | solution.py:250
  117.2 2.6 %shard_map.102 = (f32[1024,128]{1,0:T(8,128)S(1)}, f32[1024,128]{1,0:T(8,128)S(1)}) custom-call(s32[4]{0:T(128)S(1)} %get-tuple-element.48.where_ref, bf16[1024,128]{1,0:T(8,128)(2,1)S(1)} %bitcast.21, bf16[512,256]{1,0:T(8,128)(2,1)S(1)} %collective-permute-done.12.kv_ref, f32[1024,128]{1,0:T(8,128)S(1)} %get-tuple-element.28.refs_0_, ...), custom_call_target="tpu_custom_call" | custom-call | flops 1000000000 | bytes 3000000 | tf_op jit(solution)/shard_map/pallas_call | solution.py:242
  119.8 2.6 %shard_map.103 = (f32[1024,128]{1,0:T(8,128)S(1)}, f32[1024,128]{1,0:T(8,128)S(1)}) custom-call(s32[4]{0:T(128)S(1)} %get-tuple-element.47.where_ref, bf16[1024,128]{1,0:T(8,128)(2,1)S(1)} %bitcast.22, bf16[512,256]{1,0:T(8,128)(2,1)S(1)} %collective-permute-done.13.kv_ref, f32[1024,128]{1,0:T(8,128)S(1)} %get-tuple-element.30.refs_0_, ...), custom_call_target="tpu_custom_call" | custom-call | flops 1000000000 | bytes 3000000 | tf_op jit(solution)/shard_map/pallas_call | solution.py:242
  122.5 2.6 %shard_map.104 = (f32[1024,128]{1,0:T(8,128)S(1)}, f32[1024,128]{1,0:T(8,128)S(1)}) custom-call(s32[4]{0:T(128)S(1)} %get-tuple-element.46.where_ref, bf16[1024,128]{1,0:T(8,128)(2,1)S(1)} %bitcast.23, bf16[512,256]{1,0:T(8,128)(2,1)S(1)} %collective-permute-done.14.kv_ref, f32[1024,128]{1,0:T(8,128)S(1)} %get-tuple-element.32.refs_0_, ...), custom_call_target="tpu_custom_call" | custom-call | flops 1000000000 | bytes 3000000 | tf_op jit(solution)/shard_map/pallas_call | solution.py:242
  125.1 3.3 %shard_map.105 = bf16[1024,128]{1,0:T(8,128)(2,1)} custom-call(s32[4]{0:T(128)S(1)} %get-tuple-element.52.where_ref, bf16[1024,128]{1,0:T(8,128)(2,1)S(1)} %bitcast.24, bf16[512,256]{1,0:T(8,128)(2,1)S(1)} %collective-permute-done.15.kv_ref, f32[1024,128]{1,0:T(8,128)S(1)} %get-tuple-element.34.refs_0_, f32[1024,128]{1,0:T(8,128)S(1)} %get-tuple-element.35.refs_1_), custom_call_target="tpu_custom_call" | custom-call | flops 1000000000 | bytes 3000000 | tf_op jit(solution)/shard_map/pallas_call | solution.py:242
  (59 shorter events, 6.2 us)
Async XLA Ops:
  1.4 29.6 %collective-permute-start.6 = (bf16[128,256]{1,0:T(8,128)(2,1)S(1)}, bf16[128,256]{1,0:T(8,128)(2,1)S(1)}, u32[]{:S(2)}, u32[]{:S(2)}) collective-permute-start(bf16[128,256]{1,0:T(8,128)(2,1)S(1)} %pad_maximum_fusion.1), channel_id=1, source_target_pairs={{0,48},{48,96},{96,144},{1,49},{49,97},{97,145},{2,50},{50,98},{98... | collective-permute-start | bytes 196616 | tf_op jit(solution)/shard_map/ppermute | solution.py:189
  10.5 20.5 %collective-permute-start.7 = (bf16[128,256]{1,0:T(8,128)(2,1)S(1)}, bf16[128,256]{1,0:T(8,128)(2,1)S(1)}, u32[]{:S(2)}, u32[]{:S(2)}) collective-permute-start(bf16[128,256]{1,0:T(8,128)(2,1)S(1)} %pad_maximum_fusion.1), channel_id=1, source_target_pairs={{0,96},{48,144},{1,97},{49,145},{2,98},{50,146},{3,99},{51,147},{4... | collective-permute-start | bytes 196616 | tf_op jit(solution)/shard_map/ppermute | solution.py:189
  19.4 11.6 %collective-permute-start.8 = (bf16[128,256]{1,0:T(8,128)(2,1)S(1)}, bf16[128,256]{1,0:T(8,128)(2,1)S(1)}, u32[]{:S(2)}, u32[]{:S(2)}) collective-permute-start(bf16[128,256]{1,0:T(8,128)(2,1)S(1)} %pad_maximum_fusion.1), channel_id=1, source_target_pairs={{0,144},{1,145},{2,146},{3,147},{4,148},{5,149},{6,150},{7,151},{8... | collective-permute-start | bytes 196616 | tf_op jit(solution)/shard_map/ppermute | solution.py:189
  20.7 3.4 %copy-start.4 = (f32[16,48]{1,0:T(8,128)S(1)}, f32[16,48]{1,0:T(8,128)}, u32[]{:S(2)}) copy-start(f32[16,48]{1,0:T(8,128)} %param.11) | copy-start | bytes 9220
  21.5 5.8 %collective-permute-start = (bf16[3,8,768]{2,1,0:T(8,128)(2,1)S(1)}, bf16[3,8,768]{2,1,0:T(8,128)(2,1)S(1)}, u32[]{:S(2)}, u32[]{:S(2)}) collective-permute-start(bf16[3,8,768]{2,1,0:T(8,128)(2,1)S(1)} %slice.4), channel_id=1, source_target_pairs={{0,6},{6,12},{12,18},{18,24},{24,30},{30,36},{36,42},{42,48},{48,5... | collective-permute-start | bytes 110600 | tf_op jit(solution)/shard_map/ppermute | solution.py:194
  24.3 0.7 copy-start.5
  25.6 1.6 %copy-start = (bf16[128,3,768]{2,0,1:T(8,128)(2,1)S(1)}, bf16[128,3,768]{2,0,1:T(8,128)(2,1)}, u32[]{:S(2)}) copy-start(bf16[128,3,768]{2,0,1:T(8,128)(2,1)} %param.8) | copy-start | bytes 1769476
  28.3 2.7 %copy-start.2 = (bf16[128,1,128]{2,0,1:T(8,128)(2,1)S(1)}, bf16[128,1,128]{2,0,1:T(8,128)(2,1)}, u32[]{:S(2)}) copy-start(bf16[128,1,128]{2,0,1:T(8,128)(2,1)} %param.15) | copy-start | bytes 98308
  28.3 2.7 %copy-start.3 = (bf16[128,1,128]{2,0,1:T(8,128)(2,1)S(1)}, bf16[128,1,128]{2,0,1:T(8,128)(2,1)}, u32[]{:S(2)}) copy-start(bf16[128,1,128]{2,0,1:T(8,128)(2,1)} %param.14) | copy-start | bytes 98308
  28.4 9.9 %collective-permute-start.1 = (f32[16,768]{1,0:T(8,128)S(1)}, f32[16,768]{1,0:T(8,128)S(1)}, u32[]{:S(2)}, u32[]{:S(2)}) collective-permute-start(f32[16,768]{1,0:T(8,128)S(1)} %multiply_add_fusion.8), channel_id=1, source_target_pairs={{0,6},{6,12},{12,18},{18,24},{24,30},{30,36},{36,42},{42,48},{48,5... | collective-permute-start | bytes 147464 | tf_op jit(solution)/shard_map/ppermute | solution.py:215
  31.1 23.1 %collective-permute-start.9 = (bf16[512,256]{1,0:T(8,128)(2,1)S(1)}, bf16[512,256]{1,0:T(8,128)(2,1)S(1)}, u32[]{:S(2)}, u32[]{:S(2)}) collective-permute-start(bf16[512,256]{1,0:T(8,128)(2,1)S(1)} %pad_maximum_fusion.kv_ref), channel_id=1, source_target_pairs={{0,6},{1,43},{2,8},{3,45},{4,10},{5,47},{6,12},{7,1},{8,14},{9,3},... | collective-permute-start | bytes 786440 | tf_op jit(solution)/shard_map/ppermute | solution.py:250
  38.3 11.6 %collective-permute-start.2 = (f32[16,768]{1,0:T(8,128)S(1)}, f32[16,768]{1,0:T(8,128)S(1)}, u32[]{:S(2)}, u32[]{:S(2)}) collective-permute-start(f32[16,768]{1,0:T(8,128)S(1)} %get-tuple-element.38), channel_id=1, source_target_pairs={{0,12},{6,18},{12,24},{18,30},{24,36},{30,42},{36,48},{42,54},{48,... | collective-permute-start | bytes 147464 | tf_op jit(solution)/shard_map/ppermute | solution.py:215
  50.0 9.9 %collective-permute-start.3 = (f32[16,768]{1,0:T(8,128)S(1)}, f32[16,768]{1,0:T(8,128)S(1)}, u32[]{:S(2)}, u32[]{:S(2)}) collective-permute-start(f32[16,768]{1,0:T(8,128)S(1)} %multiply_add_fusion.5), channel_id=1, source_target_pairs={{0,24},{6,30},{12,36},{18,42},{24,48},{30,54},{36,60},{42,66},{48,... | collective-permute-start | bytes 147464 | tf_op jit(solution)/shard_map/ppermute | solution.py:215
  54.2 10.6 %collective-permute-start.10 = (bf16[512,256]{1,0:T(8,128)(2,1)S(1)}, bf16[512,256]{1,0:T(8,128)(2,1)S(1)}, u32[]{:S(2)}, u32[]{:S(2)}) collective-permute-start(bf16[512,256]{1,0:T(8,128)(2,1)S(1)} %collective-permute-done.9.kv_ref), channel_id=1, source_target_pairs={{0,6},{1,43},{2,8},{3,45},{4,10},{5,47},{6,12},{7,1},{8,14},{9,3},... | collective-permute-start | bytes 786440 | tf_op jit(solution)/shard_map/ppermute | solution.py:250
  57.1 0.7 copy-start.6
  57.9 0.7 copy-start.7
  59.9 24.7 %collective-permute-start.4 = (f32[16,768]{1,0:T(8,128)S(1)}, f32[16,768]{1,0:T(8,128)S(1)}, u32[]{:S(2)}, u32[]{:S(2)}) collective-permute-start(f32[16,768]{1,0:T(8,128)S(1)} %get-tuple-element.36), channel_id=1, source_target_pairs={{0,48},{6,54},{12,60},{18,66},{24,72},{30,78},{36,84},{42,90},{48,... | collective-permute-start | bytes 147464 | tf_op jit(solution)/shard_map/ppermute | solution.py:215
  64.8 10.9 %collective-permute-start.11 = (bf16[512,256]{1,0:T(8,128)(2,1)S(1)}, bf16[512,256]{1,0:T(8,128)(2,1)S(1)}, u32[]{:S(2)}, u32[]{:S(2)}) collective-permute-start(bf16[512,256]{1,0:T(8,128)(2,1)S(1)} %collective-permute-done.10.kv_ref), channel_id=1, source_target_pairs={{0,6},{1,43},{2,8},{3,45},{4,10},{5,47},{6,12},{7,1},{8,14},{9,3},... | collective-permute-start | bytes 786440 | tf_op jit(solution)/shard_map/ppermute | solution.py:250
  73.1 14.0 %copy-start.1 = (bf16[128,8,128]{2,1,0:T(8,128)(2,1)S(1)}, bf16[128,8,128]{2,1,0:T(8,128)(2,1)}, u32[]{:S(2)}) copy-start(bf16[128,8,128]{2,1,0:T(8,128)(2,1)} %param.13) | copy-start | bytes 786436
  75.8 12.9 %collective-permute-start.12 = (bf16[512,256]{1,0:T(8,128)(2,1)S(1)}, bf16[512,256]{1,0:T(8,128)(2,1)S(1)}, u32[]{:S(2)}, u32[]{:S(2)}) collective-permute-start(bf16[512,256]{1,0:T(8,128)(2,1)S(1)} %collective-permute-done.11.kv_ref), channel_id=1, source_target_pairs={{0,6},{1,43},{2,8},{3,45},{4,10},{5,47},{6,12},{7,1},{8,14},{9,3},... | collective-permute-start | bytes 786440 | tf_op jit(solution)/shard_map/ppermute | solution.py:250
  84.6 9.6 %collective-permute-start.5 = (f32[16,768]{1,0:T(8,128)S(1)}, f32[16,768]{1,0:T(8,128)S(1)}, u32[]{:S(2)}, u32[]{:S(2)}) collective-permute-start(f32[16,768]{1,0:T(8,128)S(1)} %multiply_add_fusion.1), channel_id=1, source_target_pairs={{0,96},{6,102},{12,108},{18,114},{24,120},{30,126},{36,132},{42,13... | collective-permute-start | bytes 147464 | tf_op jit(solution)/shard_map/ppermute | solution.py:215
  88.6 9.5 %collective-permute-start.13 = (bf16[512,256]{1,0:T(8,128)(2,1)S(1)}, bf16[512,256]{1,0:T(8,128)(2,1)S(1)}, u32[]{:S(2)}, u32[]{:S(2)}) collective-permute-start(bf16[512,256]{1,0:T(8,128)(2,1)S(1)} %collective-permute-done.12.kv_ref), channel_id=1, source_target_pairs={{0,6},{1,43},{2,8},{3,45},{4,10},{5,47},{6,12},{7,1},{8,14},{9,3},... | collective-permute-start | bytes 786440 | tf_op jit(solution)/shard_map/ppermute | solution.py:250
  98.1 13.5 %collective-permute-start.14 = (bf16[512,256]{1,0:T(8,128)(2,1)S(1)}, bf16[512,256]{1,0:T(8,128)(2,1)S(1)}, u32[]{:S(2)}, u32[]{:S(2)}) collective-permute-start(bf16[512,256]{1,0:T(8,128)(2,1)S(1)} %collective-permute-done.13.kv_ref), channel_id=1, source_target_pairs={{0,6},{1,43},{2,8},{3,45},{4,10},{5,47},{6,12},{7,1},{8,14},{9,3},... | collective-permute-start | bytes 786440 | tf_op jit(solution)/shard_map/ppermute | solution.py:250
  111.6 13.5 %collective-permute-start.15 = (bf16[512,256]{1,0:T(8,128)(2,1)S(1)}, bf16[512,256]{1,0:T(8,128)(2,1)S(1)}, u32[]{:S(2)}, u32[]{:S(2)}) collective-permute-start(bf16[512,256]{1,0:T(8,128)(2,1)S(1)} %collective-permute-done.14.kv_ref), channel_id=1, source_target_pairs={{0,6},{1,43},{2,8},{3,45},{4,10},{5,47},{6,12},{7,1},{8,14},{9,3},... | collective-permute-start | bytes 786440 | tf_op jit(solution)/shard_map/ppermute | solution.py:250

commit v2 on v1

--- a/solution.py
+++ b/solution.py
@@ -50,6 +50,7 @@
     rows, width = gated_ref.shape
     pad = rim_ref.shape[1]
     taps = taps_ref.shape[0] // 3
+    modes = LANES // (LANES // GSIZE)
     row = iota((rows, LANES), 0).astype(F32)
     same = iota((LANES, LANES), 0) // GSIZE == iota((LANES, LANES), 1) // GSIZE
     for tile in range(width // LANES):
@@ -73,10 +74,14 @@
             low, gated, preferred_element_type=F32
         )
         full = jnp.where(same, full, 0.0)
-        state = full[:GSIZE]
+        state = full[:modes]
         for g in range(1, LANES // GSIZE):
-            state = state + full[g * GSIZE : (g + 1) * GSIZE]
-        state_ref[:, cols] = state
+            state = state + full[g * modes : (g + 1) * modes]
+        high, low = split(state)
+        band, half = tile // 2, slice(tile % 2 * LANES, (tile % 2 + 1) * LANES)
+        state_ref[band * modes : (band + 1) * modes, half] = high
+        band += state_ref.shape[0] // (2 * modes)
+        state_ref[band * modes : (band + 1) * modes, half] = low
 
 
 def near_kernel(gated_ref, rate_ref, res_ref, near_ref):
@@ -109,14 +114,53 @@
         near_ref[:, cols] = near
 
 
-def join_kernel(first_ref, gated_ref, near_ref, past_ref, rate_ref, res_ref, gain_ref, out_ref):
+def fold(states, rate, exponent):
+    high, low = states
+    return jnp.exp(rate * exponent) * (high.astype(F32) + low.astype(F32))
+
+
+def gather_states(where_ref, base, message, rate_ref, before, total):
+    half = rate_ref.shape[0]
+    states = (message[:half, :], message[half:, :])
+    place, origin, ring = where_ref[base + 4], where_ref[base + 5], where_ref[base + 6]
+    span = where_ref[base + 7].astype(F32)
+    rate = -rate_ref[...] * span
+    lag = jnp.maximum(place - 1 - origin, 0).astype(F32)
+    here = jnp.where(origin < place, 1.0, 0.0)
+    before = before + here * fold(states, rate, lag)
+    total = total + fold(states, rate, (ring - 1 - origin).astype(F32))
+    return before, total
+
+
+def last_states_kernel(where_ref, message_ref, sums_ref, rate_ref, before_ref, total_ref):
+    half = rate_ref.shape[0]
+    before, total = gather_states(
+        where_ref, 0, message_ref, rate_ref, sums_ref[:half, :], sums_ref[half:, :]
+    )
+    before_ref[...] = before
+    total_ref[...] = total
+
+
+def join_kernel(
+    where_ref, first_ref, gated_ref, near_ref, before_ref, *refs
+):
+    *totals, band_ref, rate_ref, res_ref, gain_ref, out_ref, past_ref = refs
     rows, width = gated_ref.shape
+    modes = GSIZE
+    span = where_ref[7].astype(F32)
+    band_rate = -band_ref[...] * span
+    past_ref[...] = before_ref[...]
+    for number, total in enumerate(totals):
+        lag = (where_ref[4] + number * where_ref[6]).astype(F32)
+        past_ref[...] += jnp.exp(band_rate * lag) * total[...]
     row = iota((rows, LANES), 0).astype(F32)
     same = iota((LANES, LANES), 0) // GSIZE == iota((LANES, LANES), 1) // GSIZE
     for tile in range(width // LANES):
         cols = slice(tile * LANES, (tile + 1) * LANES)
         coeff_high, coeff_low = split(res_ref[:, cols] * jnp.exp(-rate_ref[:, cols] * row))
-        past = jnp.concatenate([past_ref[:, cols]] * (LANES // GSIZE), 0)
+        band, half = tile // 2, slice(tile % 2 * LANES, (tile % 2 + 1) * LANES)
+        past = past_ref[band * modes : (band + 1) * modes, half]
+        past = jnp.concatenate([past] * (LANES // GSIZE), 0)
         past_high, past_low = split(jnp.where(same, past, 0.0))
         far = (
             jnp.dot(coeff_high, past_high, preferred_element_type=F32)
@@ -127,22 +171,35 @@
         out_ref[:, cols] = (first_ref[:, cols] * (far + near_ref[:, cols] + direct)).astype(BF16)
 
 
-def attend_kernel(first, last, rows, scale, where_ref, q_ref, kv_ref, *refs):
-    blocks = kv_ref.shape[0] // rows
+def attend_kernel(first, last, rows, blocks, scale, where_ref, q_ref, *refs):
     heads = q_ref.shape[0] // rows
+    per = blocks + 4
+    messages = where_ref.shape[0] // per
+    kv_refs, refs = refs[:messages], refs[messages:]
     if first:
-        acc_out, ml_out = refs
+        rate_ref, acc_out, ml_out, sums_out = refs
     elif last:
         acc_in, ml_in, out_ref = refs
     else:
-        acc_in, ml_in, acc_out, ml_out = refs
-    chunk = 256
-    keys = kv_ref[:, :LANES]
-    values = jnp.concatenate([kv_ref[:, LANES:], jnp.ones((kv_ref.shape[0], LANES), BF16)], 1)
-    lane_block = iota((1, kv_ref.shape[0]), 1) // rows
-    bias = jnp.zeros((1, kv_ref.shape[0]), F32)
-    for b in range(1 if first else 0, blocks):
-        bias = bias + jnp.where((lane_block == b) & (where_ref[b] == 0), -1e30, 0.0)
+        rate_ref, acc_in, ml_in, sums_in, acc_out, ml_out, sums_out = refs
+    chunk = 128
+    count = blocks * rows
+    if not last:
+        half = rate_ref.shape[0]
+        zero = jnp.zeros(rate_ref.shape, F32)
+        sums = (zero, zero) if first else (sums_in[:half, :], sums_in[half:, :])
+        for number, kv_ref in enumerate(kv_refs):
+            sums = gather_states(where_ref, number * per, kv_ref[count:, :], rate_ref, *sums)
+        sums_out[:half, :], sums_out[half:, :] = sums
+    keys = jnp.concatenate([kv_ref[:count, :LANES] for kv_ref in kv_refs], 0)
+    values = jnp.concatenate([kv_ref[:count, LANES:] for kv_ref in kv_refs], 0)
+    values = jnp.concatenate([values, jnp.ones_like(values)], 1)
+    lane_block = iota((1, messages * count), 1) // rows
+    bias = jnp.zeros((1, messages * count), F32)
+    for number in range(messages):
+        for b in range(1 if first else 0, blocks):
+            hidden = where_ref[number * per + b] == 0
+            bias = bias + jnp.where((lane_block == number * blocks + b) & hidden, -1e30, 0.0)
 
     for number in range(q_ref.shape[0] // chunk):
         span = slice(number * chunk, (number + 1) * chunk)
@@ -179,76 +236,94 @@
     taps = short_taps.shape[0]
     modes, groups = modal_rate.shape
     heads, size = queries.shape[1:]
-    layers, ring, parts = lax.axis_size("zh"), lax.axis_size("y"), lax.axis_size("mp")
+    layers, ring = lax.axis_size("zh"), lax.axis_size("y")
     layer, place = lax.axis_index("zh"), lax.axis_index("y")
-    side = lax.axis_index("mp") % 2
     devices = layers * ring
 
     kv = jnp.concatenate([keys[:, 0], values[:, 0]], axis=1)
     held = [kv] + [
         lax.ppermute(kv, "zh", [(z, z + s) for z in range(layers - s)]) for s in range(1, layers)
     ]
-    held = jnp.concatenate(held, axis=0)
 
     by_kind = jnp.transpose(streams, (1, 0, 2))
     rim = lax.ppermute(by_kind[:, rows - 8 :], ("zh", "y"), [(i, i + 1) for i in range(devices - 1)])
     taps_full = jnp.repeat(short_taps.reshape(taps * kinds, groups), GSIZE, axis=1)
-    rate_full = jnp.repeat(modal_rate, GSIZE, axis=1)
+    bands = width // (2 * LANES)
+    band_rate = modal_rate.reshape(modes, bands, groups // bands).transpose(1, 0, 2)
+    band_rate = jnp.repeat(band_rate.reshape(bands * modes, groups // bands), GSIZE, axis=1)
     rate_row = modal_rate.T.reshape(1, groups * modes)
     res_row = modal_residue.T.reshape(1, groups * modes)
     wide = jax.ShapeDtypeStruct((rows, width), F32)
     first, gated, state = call(
         filter_kernel,
-        [wide, jax.ShapeDtypeStruct((rows, width), BF16), jax.ShapeDtypeStruct((modes, width), F32)],
+        [wide, jax.ShapeDtypeStruct((rows, width), BF16), jax.ShapeDtypeStruct((6 * modes, 2 * LANES), BF16)],
         vmem(4),
         4_000_000_000,
         4_000_000,
         [pltpu.VMEM((3, rows + 8, LANES), F32)],
     )(by_kind, rim, taps_full, rate_row)
-    near = call(near_kernel, wide, vmem(3), 4_000_000_000, 4_000_000)(gated, rate_row, res_row)
-
-    past = jnp.zeros_like(state)
-    step_rate = -rate_full * float(rows)
-    step = 1
-    while step < devices:
-        full = state + jnp.exp(step_rate) * past
-        come = lax.ppermute(full, ("zh", "y"), [(i, i + step) for i in range(devices - step)])
-        past = past + jnp.exp(step_rate * (step - 1.0)) * come
-        step *= 2
+
+    rows_q = queries.reshape(rows * heads, size)
+    scale = LOG2E / math.sqrt(size)
+    state_shape = [jax.ShapeDtypeStruct((rows * heads, LANES), F32)] * 2
+    sums_shape = jax.ShapeDtypeStruct((2 * bands * modes, 2 * LANES), F32)
+    band_shape = jax.ShapeDtypeStruct((bands * modes, 2 * LANES), F32)
+    layer_seen = (layer >= jnp.arange(1, layers)).astype(jnp.int32)
+
+    def describe(offset):
+        origin = (place + offset) % ring
+        return jnp.concatenate(
+            [
+                (origin < place)[None].astype(jnp.int32),
+                layer_seen,
+                jnp.stack([place, origin, jnp.int32(ring), jnp.int32(rows)]),
+            ]
+        )
+
+    def attend(messages, offsets, carry, first=False, last=False):
+        where = jnp.concatenate([describe(offset) for offset in offsets])
+        return call(
+            functools.partial(attend_kernel, first, last, rows, layers, scale),
+            jax.ShapeDtypeStruct((rows * heads, size), BF16) if last else state_shape + [sums_shape],
+            [smem()] + vmem(1 + len(messages) + len(carry)),
+            1_000_000_000 * len(messages),
+            3_000_000,
+        )(where, rows_q, *messages, *carry)
+
+    def turn(message, by):
+        return lax.ppermute(message, "y", [(y, (y + by) % ring) for y in range(ring)])
+
+    message = jnp.concatenate(held + [state], axis=0)
+    pending, offsets, carry = [message], [0], (band_rate,)
+    for step in range(1, ring // 2 + 1):
+        both = 2 * step < ring
+        sent = [turn(pending[0], 1)] + ([turn(pending[-1], -1)] if both else [])
+        carry = attend(pending, offsets, carry, first=step == 1)
+        if step == 1:
+            near = call(near_kernel, wide, vmem(3), 4_000_000_000, 4_000_000)(
+                gated, rate_row, res_row
+            )
+            *sent, near = lax.optimization_barrier((*sent, near))
+        *sent, acc, highest, sums = lax.optimization_barrier((*sent, *carry))
+        carry = (band_rate, acc, highest, sums)
+        pending, offsets = sent, ([-step, step] if both else [-step])
+    where = describe(offsets[0])
+    before, total = call(
+        last_states_kernel, [band_shape] * 2, [smem()] + vmem(3), 1_000_000, 500_000
+    )(where, pending[0][layers * rows :], sums, band_rate)
+    attn_out = attend(pending, offsets, (acc, highest), last=True).reshape(rows, heads, size)
+
+    totals = [
+        lax.ppermute(total, "zh", [(z, z + s) for z in range(layers - s)]) for s in range(1, layers)
+    ]
     hyena_out = call(
         join_kernel,
         jax.ShapeDtypeStruct((rows, width), BF16),
-        vmem(7),
+        [smem()] + vmem(8 + len(totals)),
         500_000_000,
         2_000_000,
-    )(first, gated, near, past, rate_row, res_row, skip_gain.reshape(1, width))
-
-    rows_q = queries.reshape(rows * heads, size)
-    scale = LOG2E / math.sqrt(size)
-    pairs = [
-        (y * parts + m, ((y + (1 if m % 2 == 0 else -1)) % ring) * parts + m)
-        for y in range(ring)
-        for m in range(parts)
-    ]
-    state_shape = [jax.ShapeDtypeStruct((rows * heads, LANES), F32)] * 2
-    carry = ()
-    attn_out = None
-    for step in range(ring):
-        origin = (place + jnp.where(side == 0, -step, step)) % ring
-        visible = jnp.concatenate(
-            [(origin < place)[None], layer >= jnp.arange(1, layers)]
-        ).astype(jnp.int32)
-        last = step == ring - 1
-        carry = call(
-            functools.partial(attend_kernel, step == 0, last, rows, scale),
-            jax.ShapeDtypeStruct((rows * heads, size), BF16) if last else state_shape,
-            [smem()] + vmem(2 + len(carry)),
-            1_000_000_000,
-            3_000_000,
-        )(visible, rows_q, held, *carry)
-        if not last:
-            held = lax.ppermute(held, ("y", "mp"), pairs)
-    attn_out = carry.reshape(rows, heads, size)
+        [pltpu.VMEM((bands * modes, 2 * LANES), F32)],
+    )(where, first, gated, near, before, *totals, band_rate, rate_row, res_row, skip_gain.reshape(1, width))
     return hyena_out, attn_out
 
 

time: 129 us -> 104 us (0.81)
  the two profiles are of different devices: /device:TPU:178 before, /device:TPU:6 now
where the time goes in v2:
time: 104 us; the launch traced here: 103 us
  starting transfers between devices  64.1 us (62%)
  Pallas kernels  20.2 us (19%)
  local copies, waits for them, and re-layouts  13 us (12%)
  waiting for transfers between devices  3.52 us (3%)
  between operations  1.12 us (1%)
    ppermute x7, starting transfers between devices, turn(): lax.ppermute(message, 'y', [(y, (y + by) % ring) for y in range(ring)])  24.1 us
    ppermute x3, starting transfers between devices, body(): lax.ppermute(kv, 'zh', [(z, z + s) for z in range(layers - s)])  22.2 us
    ppermute x3, starting transfers between devices, body(): lax.ppermute(total, 'zh', [(z, z + s) for z in range(layers - s)])  14.2 us
    pallas_call x5, Pallas kernels, attend(): call(functools.partial(attend_kernel, first, last, rows, layers, scale),...  13.6 us
    unnamed x36, local copies, waits for them, and re-layouts  10.7 us
    ppermute x7, waiting for transfers between devices, turn(): lax.ppermute(message, 'y', [(y, (y + by) % ring) for y in range(ring)])  3.5 us
    ppermute x1, starting transfers between devices, body(): lax.ppermute(by_kind[:, rows - 8:], ('zh', 'y'), [(i, i + 1) for i in ran...  3.47 us
    pallas_call x1, Pallas kernels, body(): call(near_kernel, wide, vmem(3), 4000000000, 4000000)  3.39 us
  transfers between devices with their start and end apart: 14, of which 3 were waited for; matrix products, arithmetic and copies ran while one was open for 2% of the time, Pallas kernels for 18%

profile of v2, /device:TPU:6, one launch (start us, length us, event | category | flops | bytes accessed | tf_op | source)
XLA Modules:
  0.0 102.6 jit_solution(11988051883965687597)
XLA Ops:
  1.4 7.9 %collective-permute-start.1 = (bf16[128,256]{1,0:T(8,128)(2,1)S(1)}, bf16[128,256]{1,0:T(8,128)(2,1)S(1)}, u32[]{:S(2)}, u32[]{:S(2)}) collective-permute-start(bf16[128,256]{1,0:T(8,128)(2,1)S(1)} %get-tuple-element.80), channel_id=1, source_target_pairs={{0,48},{48,96},{96,144},{1,49},{49,97},{97,145},{2,50},{50,98},{98... | collective-permute-start | bytes 196616 | tf_op jit(solution)/shard_map/ppermute | solution.py:245
  9.3 13.0 %collective-permute-start.2 = (bf16[128,256]{1,0:T(8,128)(2,1)S(1)}, bf16[128,256]{1,0:T(8,128)(2,1)S(1)}, u32[]{:S(2)}, u32[]{:S(2)}) collective-permute-start(bf16[128,256]{1,0:T(8,128)(2,1)S(1)} %get-tuple-element.80), channel_id=1, source_target_pairs={{0,96},{48,144},{1,97},{49,145},{2,98},{50,146},{3,99},{51,147},{4... | collective-permute-start | bytes 196616 | tf_op jit(solution)/shard_map/ppermute | solution.py:245
  22.4 1.3 %collective-permute-start.3 = (bf16[128,256]{1,0:T(8,128)(2,1)S(1)}, bf16[128,256]{1,0:T(8,128)(2,1)S(1)}, u32[]{:S(2)}, u32[]{:S(2)}) collective-permute-start(bf16[128,256]{1,0:T(8,128)(2,1)S(1)} %get-tuple-element.80), channel_id=1, source_target_pairs={{0,144},{1,145},{2,146},{3,147},{4,148},{5,149},{6,150},{7,151},{8... | collective-permute-start | bytes 196616 | tf_op jit(solution)/shard_map/ppermute | solution.py:245
  24.5 3.5 %collective-permute-start = (bf16[3,8,768]{2,1,0:T(8,128)(2,1)S(1)}, bf16[3,8,768]{2,1,0:T(8,128)(2,1)S(1)}, u32[]{:S(2)}, u32[]{:S(2)}) collective-permute-start(bf16[3,8,768]{2,1,0:T(8,128)(2,1)S(1)} %slice.8), channel_id=1, source_target_pairs={{0,6},{6,12},{12,18},{18,24},{24,30},{30,36},{36,42},{42,48},{48,5... | collective-permute-start | bytes 110600 | tf_op jit(solution)/shard_map/ppermute | solution.py:249
  31.2 1.0 shard_map.95
  32.3 3.5 %collective-permute-start.4 = (bf16[608,256]{1,0:T(8,128)(2,1)S(1)}, bf16[608,256]{1,0:T(8,128)(2,1)S(1)}, u32[]{:S(2)}, u32[]{:S(2)}) collective-permute-start(bf16[608,256]{1,0:T(8,128)(2,1)S(1)} %constant_dynamic-update-slice_fusion.refs_0_), channel_id=1, source_target_pairs={{0,6},{6,12},{12,18},{18,24},{24,30},{30,36},{36,42},{42,0},{1,7},... | collective-permute-start | bytes 933896 | tf_op jit(solution)/shard_map/ppermute | solution.py:294
  35.8 3.6 %collective-permute-start.5 = (bf16[608,256]{1,0:T(8,128)(2,1)S(1)}, bf16[608,256]{1,0:T(8,128)(2,1)S(1)}, u32[]{:S(2)}, u32[]{:S(2)}) collective-permute-start(bf16[608,256]{1,0:T(8,128)(2,1)S(1)} %constant_dynamic-update-slice_fusion.refs_0_), channel_id=1, source_target_pairs={{0,42},{6,0},{12,6},{18,12},{24,18},{30,24},{36,30},{42,36},{1,43}... | collective-permute-start | bytes 933896 | tf_op jit(solution)/shard_map/ppermute | solution.py:294
  39.4 3.4 %shard_map.96.near_ref = f32[128,768]{1,0:T(8,128)S(1)} custom-call(bf16[128,768]{1,0:T(8,128)(2,1)S(1)} %get-tuple-element.42.gated_ref, f32[1,768]{1,0:T(1,128)S(1)} %reshape.52.rate_ref.refs_4_, f32[1,768]{1,0:T(1,128)S(1)} %reshape.53.res_ref.refs_5_), custom_call_target="tpu_custom_call" | custom-call | flops 4000000000 | bytes 4000000 | tf_op jit(solution)/shard_map/pallas_call | solution.py:303
  42.8 1.6 %shard_map.97 = (f32[1024,128]{1,0:T(8,128)S(1)}, f32[1024,128]{1,0:T(8,128)S(1)}, f32[96,256]{1,0:T(8,128)S(1)}) custom-call(s32[8]{0:T(128)S(1)} %concatenate.25.where_ref, bf16[1024,128]{1,0:T(8,128)(2,1)S(1)} %bitcast.30, bf16[608,256]{1,0:T(8,128)(2,1)S(1)} %constant_dynamic-update-slice_fusion.refs_0_, f32[48,256]{1,0:T(8,128)S(1)} %copy.16.refs_1_.refs_2_.rate_ref.refs_3_), custom_call_target="tpu_custom_call" | custom-call | flops 1000000000 | bytes 3000000 | tf_op jit(solution)/shard_map/pallas_call | solution.py:285
  44.3 0.8 copy-done.2
  45.6 4.5 %collective-permute-start.6 = (bf16[608,256]{1,0:T(8,128)(2,1)S(1)}, bf16[608,256]{1,0:T(8,128)(2,1)S(1)}, u32[]{:S(2)}, u32[]{:S(2)}) collective-permute-start(bf16[608,256]{1,0:T(8,128)(2,1)S(1)} %collective-permute-done.4.refs_0_), channel_id=1, source_target_pairs={{0,6},{6,12},{12,18},{18,24},{24,30},{30,36},{36,42},{42,0},{1,7},... | collective-permute-start | bytes 933896 | tf_op jit(solution)/shard_map/ppermute | solution.py:294
  50.2 2.5 %collective-permute-start.7 = (bf16[608,256]{1,0:T(8,128)(2,1)S(1)}, bf16[608,256]{1,0:T(8,128)(2,1)S(1)}, u32[]{:S(2)}, u32[]{:S(2)}) collective-permute-start(bf16[608,256]{1,0:T(8,128)(2,1)S(1)} %collective-permute-done.5.refs_1_), channel_id=1, source_target_pairs={{0,42},{6,0},{12,6},{18,12},{24,18},{30,24},{36,30},{42,36},{1,43}... | collective-permute-start | bytes 933896 | tf_op jit(solution)/shard_map/ppermute | solution.py:294
  52.8 1.0 %copy-done.3 = f32[1024,128]{1,0:T(8,128)S(1)} copy-done((f32[1024,128]{1,0:T(8,128)S(1)}, f32[1024,128]{1,0:T(8,128)}, u32[]{:S(2)}) %copy-start.3) | copy-done | bytes 524312
  53.9 2.8 %shard_map.98 = (f32[1024,128]{1,0:T(8,128)S(1)}, f32[1024,128]{1,0:T(8,128)S(1)}, f32[96,256]{1,0:T(8,128)S(1)}) custom-call(s32[16]{0:T(128)S(1)} %concatenate.26.where_ref, bf16[1024,128]{1,0:T(8,128)(2,1)S(1)} %bitcast.31, bf16[608,256]{1,0:T(8,128)(2,1)S(1)} %collective-permute-done.4.refs_0_, bf16[608,256]{1,0:T(8,128)(2,1)S(1)} %collective-permute-done.5.refs_1_, ...), custom_call_target="tpu_custom_call" | custom-call | flops 2000000000 | bytes 3000000 | tf_op jit(solution)/shard_map/pallas_call | solution.py:285
  56.7 0.8 copy-done.6
  57.5 0.8 copy-done.8
  58.3 0.8 collective-permute-done.7.refs_1_
  59.1 3.7 %collective-permute-start.8 = (bf16[608,256]{1,0:T(8,128)(2,1)S(1)}, bf16[608,256]{1,0:T(8,128)(2,1)S(1)}, u32[]{:S(2)}, u32[]{:S(2)}) collective-permute-start(bf16[608,256]{1,0:T(8,128)(2,1)S(1)} %collective-permute-done.6.refs_0_), channel_id=1, source_target_pairs={{0,6},{6,12},{12,18},{18,24},{24,30},{30,36},{36,42},{42,0},{1,7},... | collective-permute-start | bytes 933896 | tf_op jit(solution)/shard_map/ppermute | solution.py:294
  62.9 3.3 %collective-permute-start.9 = (bf16[608,256]{1,0:T(8,128)(2,1)S(1)}, bf16[608,256]{1,0:T(8,128)(2,1)S(1)}, u32[]{:S(2)}, u32[]{:S(2)}) collective-permute-start(bf16[608,256]{1,0:T(8,128)(2,1)S(1)} %collective-permute-done.7.refs_1_), channel_id=1, source_target_pairs={{0,42},{6,0},{12,6},{18,12},{24,18},{30,24},{36,30},{42,36},{1,43}... | collective-permute-start | bytes 933896 | tf_op jit(solution)/shard_map/ppermute | solution.py:294
  67.0 1.0 %copy-done.7 = f32[1024,128]{1,0:T(8,128)S(1)} copy-done((f32[1024,128]{1,0:T(8,128)S(1)}, f32[1024,128]{1,0:T(8,128)}, u32[]{:S(2)}) %copy-start.7) | copy-done | bytes 524312
  68.0 1.0 %copy-done.9 = f32[1024,128]{1,0:T(8,128)S(1)} copy-done((f32[1024,128]{1,0:T(8,128)S(1)}, f32[1024,128]{1,0:T(8,128)}, u32[]{:S(2)}) %copy-start.9) | copy-done | bytes 524312
  69.0 2.9 %shard_map.99 = (f32[1024,128]{1,0:T(8,128)S(1)}, f32[1024,128]{1,0:T(8,128)S(1)}, f32[96,256]{1,0:T(8,128)S(1)}) custom-call(s32[16]{0:T(128)S(1)} %concatenate.27.where_ref, bf16[1024,128]{1,0:T(8,128)(2,1)S(1)} %bitcast.32, bf16[608,256]{1,0:T(8,128)(2,1)S(1)} %collective-permute-done.6.refs_0_, bf16[608,256]{1,0:T(8,128)(2,1)S(1)} %collective-permute-done.7.refs_1_, ...), custom_call_target="tpu_custom_call" | custom-call | flops 2000000000 | bytes 3000000 | tf_op jit(solution)/shard_map/pallas_call | solution.py:285
  71.9 0.8 copy-done.4
  72.7 3.0 %collective-permute-start.10 = (bf16[608,256]{1,0:T(8,128)(2,1)S(1)}, bf16[608,256]{1,0:T(8,128)(2,1)S(1)}, u32[]{:S(2)}, u32[]{:S(2)}) collective-permute-start(bf16[608,256]{1,0:T(8,128)(2,1)S(1)} %collective-permute-done.8.refs_0_), channel_id=1, source_target_pairs={{0,6},{6,12},{12,18},{18,24},{24,30},{30,36},{36,42},{42,0},{1,7},... | collective-permute-start | bytes 933896 | tf_op jit(solution)/shard_map/ppermute | solution.py:294
  76.7 1.0 %copy-done.5 = f32[1024,128]{1,0:T(8,128)S(1)} copy-done((f32[1024,128]{1,0:T(8,128)S(1)}, f32[1024,128]{1,0:T(8,128)}, u32[]{:S(2)}) %copy-start.5) | copy-done | bytes 524312
  77.7 2.8 %shard_map.100 = (f32[1024,128]{1,0:T(8,128)S(1)}, f32[1024,128]{1,0:T(8,128)S(1)}, f32[96,256]{1,0:T(8,128)S(1)}) custom-call(s32[16]{0:T(128)S(1)} %concatenate.28.where_ref, bf16[1024,128]{1,0:T(8,128)(2,1)S(1)} %bitcast.33, bf16[608,256]{1,0:T(8,128)(2,1)S(1)} %collective-permute-done.8.refs_0_, bf16[608,256]{1,0:T(8,128)(2,1)S(1)} %collective-permute-done.9.refs_1_, ...), custom_call_target="tpu_custom_call" | custom-call | flops 2000000000 | bytes 3000000 | tf_op jit(solution)/shard_map/pallas_call | solution.py:285
  80.5 2.2 %collective-permute-done.10.refs_0_ = bf16[608,256]{1,0:T(8,128)(2,1)S(1)} collective-permute-done((bf16[608,256]{1,0:T(8,128)(2,1)S(1)}, bf16[608,256]{1,0:T(8,128)(2,1)S(1)}, u32[]{:S(2)}, u32[]{:S(2)}) %collective-permute-start.10) | collective-permute-done | bytes 311328 | tf_op jit(solution)/shard_map/ppermute | solution.py:294
  83.3 4.5 %collective-permute-start.11 = (f32[48,256]{1,0:T(8,128)S(1)}, f32[48,256]{1,0:T(8,128)S(1)}, u32[]{:S(2)}, u32[]{:S(2)}) collective-permute-start(f32[48,256]{1,0:T(8,128)S(1)} %get-tuple-element.77), channel_id=1, source_target_pairs={{0,48},{48,96},{96,144},{1,49},{49,97},{97,145},{2,50},{50,98},{98... | collective-permute-start | bytes 147464 | tf_op jit(solution)/shard_map/ppermute | solution.py:317
  87.8 8.5 %collective-permute-start.12 = (f32[48,256]{1,0:T(8,128)S(1)}, f32[48,256]{1,0:T(8,128)S(1)}, u32[]{:S(2)}, u32[]{:S(2)}) collective-permute-start(f32[48,256]{1,0:T(8,128)S(1)} %get-tuple-element.77), channel_id=1, source_target_pairs={{0,96},{48,144},{1,97},{49,145},{2,98},{50,146},{3,99},{51,147},{4... | collective-permute-start | bytes 147464 | tf_op jit(solution)/shard_map/ppermute | solution.py:317
  96.2 1.3 %collective-permute-start.13 = (f32[48,256]{1,0:T(8,128)S(1)}, f32[48,256]{1,0:T(8,128)S(1)}, u32[]{:S(2)}, u32[]{:S(2)}) collective-permute-start(f32[48,256]{1,0:T(8,128)S(1)} %get-tuple-element.77), channel_id=1, source_target_pairs={{0,144},{1,145},{2,146},{3,147},{4,148},{5,149},{6,150},{7,151},{8... | collective-permute-start | bytes 147464 | tf_op jit(solution)/shard_map/ppermute | solution.py:317
  97.5 3.5 %shard_map.103 = bf16[1024,128]{1,0:T(8,128)(2,1)} custom-call(s32[8]{0:T(128)S(1)} %concatenate.22.where_ref, bf16[1024,128]{1,0:T(8,128)(2,1)S(1)} %bitcast.34, bf16[608,256]{1,0:T(8,128)(2,1)S(1)} %collective-permute-done.10.refs_0_, f32[1024,128]{1,0:T(8,128)S(1)} %get-tuple-element.78.refs_1_, f32[1024,128]{1,0:T(8,128)S(1)} %get-tuple-element.79.refs_2_), custom_call_target="tpu_custom_call" | custom-call | flops 1000000000 | bytes 3000000 | tf_op jit(solution)/shard_map/pallas_call | solution.py:285
  101.0 1.6 %shard_map.102 = bf16[128,768]{1,0:T(8,128)(2,1)} custom-call(s32[8]{0:T(128)S(1)} %concatenate.22.where_ref, f32[128,768]{1,0:T(8,128)S(1)} %get-tuple-element.41.first_ref, bf16[128,768]{1,0:T(8,128)(2,1)S(1)} %get-tuple-element.42.gated_ref, f32[128,768]{1,0:T(8,128)S(1)} %shard_map.96.near_ref, f32[48,256]{1,0:T(8,128)S(1)} %get-tuple-element.76.before_ref, ...), custom_call_target="tpu_custom_call" | custom-call | flops 500000000 | bytes 2000000 | tf_op jit(solution)/shard_map/pallas_call | solution.py:319
  (64 shorter events, 7.5 us)
Async XLA Ops:
  1.4 30.8 %collective-permute-start.1 = (bf16[128,256]{1,0:T(8,128)(2,1)S(1)}, bf16[128,256]{1,0:T(8,128)(2,1)S(1)}, u32[]{:S(2)}, u32[]{:S(2)}) collective-permute-start(bf16[128,256]{1,0:T(8,128)(2,1)S(1)} %get-tuple-element.80), channel_id=1, source_target_pairs={{0,48},{48,96},{96,144},{1,49},{49,97},{97,145},{2,50},{50,98},{98... | collective-permute-start | bytes 196616 | tf_op jit(solution)/shard_map/ppermute | solution.py:245
  9.3 22.9 %collective-permute-start.2 = (bf16[128,256]{1,0:T(8,128)(2,1)S(1)}, bf16[128,256]{1,0:T(8,128)(2,1)S(1)}, u32[]{:S(2)}, u32[]{:S(2)}) collective-permute-start(bf16[128,256]{1,0:T(8,128)(2,1)S(1)} %get-tuple-element.80), channel_id=1, source_target_pairs={{0,96},{48,144},{1,97},{49,145},{2,98},{50,146},{3,99},{51,147},{4... | collective-permute-start | bytes 196616 | tf_op jit(solution)/shard_map/ppermute | solution.py:245
  22.4 9.9 %collective-permute-start.3 = (bf16[128,256]{1,0:T(8,128)(2,1)S(1)}, bf16[128,256]{1,0:T(8,128)(2,1)S(1)}, u32[]{:S(2)}, u32[]{:S(2)}) collective-permute-start(bf16[128,256]{1,0:T(8,128)(2,1)S(1)} %get-tuple-element.80), channel_id=1, source_target_pairs={{0,144},{1,145},{2,146},{3,147},{4,148},{5,149},{6,150},{7,151},{8... | collective-permute-start | bytes 196616 | tf_op jit(solution)/shard_map/ppermute | solution.py:245
  24.5 6.7 %collective-permute-start = (bf16[3,8,768]{2,1,0:T(8,128)(2,1)S(1)}, bf16[3,8,768]{2,1,0:T(8,128)(2,1)S(1)}, u32[]{:S(2)}, u32[]{:S(2)}) collective-permute-start(bf16[3,8,768]{2,1,0:T(8,128)(2,1)S(1)} %slice.8), channel_id=1, source_target_pairs={{0,6},{6,12},{12,18},{18,24},{24,30},{30,36},{36,42},{42,48},{48,5... | collective-permute-start | bytes 110600 | tf_op jit(solution)/shard_map/ppermute | solution.py:249
  28.0 24.8 %copy-start.11 = (s32[3]{0:T(128)}, s32[3]{0:T(128)S(1)}, u32[]{:S(2)}) copy-start(s32[3]{0:T(128)S(1)} %compare_convert_fusion) | copy-start | bytes 40
  28.0 0.7 copy-start.10
  28.8 0.7 copy-start.13
  29.8 1.4 %copy-start = (bf16[128,3,768]{2,0,1:T(8,128)(2,1)S(1)}, bf16[128,3,768]{2,0,1:T(8,128)(2,1)}, u32[]{:S(2)}) copy-start(bf16[128,3,768]{2,0,1:T(8,128)(2,1)} %param.8) | copy-start | bytes 1769476
  30.2 0.7 copy-start.14
  32.3 12.9 %collective-permute-start.4 = (bf16[608,256]{1,0:T(8,128)(2,1)S(1)}, bf16[608,256]{1,0:T(8,128)(2,1)S(1)}, u32[]{:S(2)}, u32[]{:S(2)}) collective-permute-start(bf16[608,256]{1,0:T(8,128)(2,1)S(1)} %constant_dynamic-update-slice_fusion.refs_0_), channel_id=1, source_target_pairs={{0,6},{6,12},{12,18},{18,24},{24,30},{30,36},{36,42},{42,0},{1,7},... | collective-permute-start | bytes 933896 | tf_op jit(solution)/shard_map/ppermute | solution.py:294
  35.8 9.9 %collective-permute-start.5 = (bf16[608,256]{1,0:T(8,128)(2,1)S(1)}, bf16[608,256]{1,0:T(8,128)(2,1)S(1)}, u32[]{:S(2)}, u32[]{:S(2)}) collective-permute-start(bf16[608,256]{1,0:T(8,128)(2,1)S(1)} %constant_dynamic-update-slice_fusion.refs_0_), channel_id=1, source_target_pairs={{0,42},{6,0},{12,6},{18,12},{24,18},{30,24},{36,30},{42,36},{1,43}... | collective-permute-start | bytes 933896 | tf_op jit(solution)/shard_map/ppermute | solution.py:294
  39.3 3.4 %copy-start.1 = (bf16[128,8,128]{2,1,0:T(8,128)(2,1)S(1)}, bf16[128,8,128]{2,1,0:T(8,128)(2,1)}, u32[]{:S(2)}) copy-start(bf16[128,8,128]{2,1,0:T(8,128)(2,1)} %param.13) | copy-start | bytes 786436
  44.3 0.8 copy-start.2
  45.6 12.7 %collective-permute-start.6 = (bf16[608,256]{1,0:T(8,128)(2,1)S(1)}, bf16[608,256]{1,0:T(8,128)(2,1)S(1)}, u32[]{:S(2)}, u32[]{:S(2)}) collective-permute-start(bf16[608,256]{1,0:T(8,128)(2,1)S(1)} %collective-permute-done.4.refs_0_), channel_id=1, source_target_pairs={{0,6},{6,12},{12,18},{18,24},{24,30},{30,36},{36,42},{42,0},{1,7},... | collective-permute-start | bytes 933896 | tf_op jit(solution)/shard_map/ppermute | solution.py:294
  50.2 8.9 %collective-permute-start.7 = (bf16[608,256]{1,0:T(8,128)(2,1)S(1)}, bf16[608,256]{1,0:T(8,128)(2,1)S(1)}, u32[]{:S(2)}, u32[]{:S(2)}) collective-permute-start(bf16[608,256]{1,0:T(8,128)(2,1)S(1)} %collective-permute-done.5.refs_1_), channel_id=1, source_target_pairs={{0,42},{6,0},{12,6},{18,12},{24,18},{30,24},{36,30},{42,36},{1,43}... | collective-permute-start | bytes 933896 | tf_op jit(solution)/shard_map/ppermute | solution.py:294
  52.8 1.0 %copy-start.3 = (f32[1024,128]{1,0:T(8,128)S(1)}, f32[1024,128]{1,0:T(8,128)}, u32[]{:S(2)}) copy-start(f32[1024,128]{1,0:T(8,128)} %copy-done.2) | copy-start | bytes 1572868
  56.7 0.8 copy-start.6
  57.5 0.8 copy-start.8
  59.1 13.6 %collective-permute-start.8 = (bf16[608,256]{1,0:T(8,128)(2,1)S(1)}, bf16[608,256]{1,0:T(8,128)(2,1)S(1)}, u32[]{:S(2)}, u32[]{:S(2)}) collective-permute-start(bf16[608,256]{1,0:T(8,128)(2,1)S(1)} %collective-permute-done.6.refs_0_), channel_id=1, source_target_pairs={{0,6},{6,12},{12,18},{18,24},{24,30},{30,36},{36,42},{42,0},{1,7},... | collective-permute-start | bytes 933896 | tf_op jit(solution)/shard_map/ppermute | solution.py:294
  62.9 9.9 %collective-permute-start.9 = (bf16[608,256]{1,0:T(8,128)(2,1)S(1)}, bf16[608,256]{1,0:T(8,128)(2,1)S(1)}, u32[]{:S(2)}, u32[]{:S(2)}) collective-permute-start(bf16[608,256]{1,0:T(8,128)(2,1)S(1)} %collective-permute-done.7.refs_1_), channel_id=1, source_target_pairs={{0,42},{6,0},{12,6},{18,12},{24,18},{30,24},{36,30},{42,36},{1,43}... | collective-permute-start | bytes 933896 | tf_op jit(solution)/shard_map/ppermute | solution.py:294
  66.2 0.7 copy-start.12
  67.0 1.0 %copy-start.7 = (f32[1024,128]{1,0:T(8,128)S(1)}, f32[1024,128]{1,0:T(8,128)}, u32[]{:S(2)}) copy-start(f32[1024,128]{1,0:T(8,128)} %copy-done.6) | copy-start | bytes 1572868
  68.0 1.0 %copy-start.9 = (f32[1024,128]{1,0:T(8,128)S(1)}, f32[1024,128]{1,0:T(8,128)}, u32[]{:S(2)}) copy-start(f32[1024,128]{1,0:T(8,128)} %copy-done.8) | copy-start | bytes 1572868
  71.9 0.8 copy-start.4
  72.7 10.0 %collective-permute-start.10 = (bf16[608,256]{1,0:T(8,128)(2,1)S(1)}, bf16[608,256]{1,0:T(8,128)(2,1)S(1)}, u32[]{:S(2)}, u32[]{:S(2)}) collective-permute-start(bf16[608,256]{1,0:T(8,128)(2,1)S(1)} %collective-permute-done.8.refs_0_), channel_id=1, source_target_pairs={{0,6},{6,12},{12,18},{18,24},{24,30},{30,36},{36,42},{42,0},{1,7},... | collective-permute-start | bytes 933896 | tf_op jit(solution)/shard_map/ppermute | solution.py:294
  75.8 0.7 copy-start.15
  76.7 1.0 %copy-start.5 = (f32[1024,128]{1,0:T(8,128)S(1)}, f32[1024,128]{1,0:T(8,128)}, u32[]{:S(2)}) copy-start(f32[1024,128]{1,0:T(8,128)} %copy-done.4) | copy-start | bytes 1572868
  83.3 17.7 %collective-permute-start.11 = (f32[48,256]{1,0:T(8,128)S(1)}, f32[48,256]{1,0:T(8,128)S(1)}, u32[]{:S(2)}, u32[]{:S(2)}) collective-permute-start(f32[48,256]{1,0:T(8,128)S(1)} %get-tuple-element.77), channel_id=1, source_target_pairs={{0,48},{48,96},{96,144},{1,49},{49,97},{97,145},{2,50},{50,98},{98... | collective-permute-start | bytes 147464 | tf_op jit(solution)/shard_map/ppermute | solution.py:317
  87.8 13.2 %collective-permute-start.12 = (f32[48,256]{1,0:T(8,128)S(1)}, f32[48,256]{1,0:T(8,128)S(1)}, u32[]{:S(2)}, u32[]{:S(2)}) collective-permute-start(f32[48,256]{1,0:T(8,128)S(1)} %get-tuple-element.77), channel_id=1, source_target_pairs={{0,96},{48,144},{1,97},{49,145},{2,98},{50,146},{3,99},{51,147},{4... | collective-permute-start | bytes 147464 | tf_op jit(solution)/shard_map/ppermute | solution.py:317
  96.2 4.8 %collective-permute-start.13 = (f32[48,256]{1,0:T(8,128)S(1)}, f32[48,256]{1,0:T(8,128)S(1)}, u32[]{:S(2)}, u32[]{:S(2)}) collective-permute-start(f32[48,256]{1,0:T(8,128)S(1)} %get-tuple-element.77), channel_id=1, source_target_pairs={{0,144},{1,145},{2,146},{3,147},{4,148},{5,149},{6,150},{7,151},{8... | collective-permute-start | bytes 147464 | tf_op jit(solution)/shard_map/ppermute | solution.py:317

commit v3 on v2

--- a/solution.py
+++ b/solution.py
@@ -32,7 +32,7 @@
         in_specs=in_specs,
         out_specs=vmem(len(out_shape)) if many else vmem(1)[0],
         scratch_shapes=list(scratch),
-        compiler_params=pltpu.CompilerParams(vmem_limit_bytes=32 * 1024 * 1024),
+        compiler_params=pltpu.CompilerParams(vmem_limit_bytes=16 * 1024 * 1024),
         cost_estimate=pl.CostEstimate(flops=flops, bytes_accessed=moved, transcendentals=0),
     )
 
@@ -299,18 +299,16 @@
         both = 2 * step < ring
         sent = [turn(pending[0], 1)] + ([turn(pending[-1], -1)] if both else [])
         carry = attend(pending, offsets, carry, first=step == 1)
-        if step == 1:
-            near = call(near_kernel, wide, vmem(3), 4_000_000_000, 4_000_000)(
-                gated, rate_row, res_row
-            )
-            *sent, near = lax.optimization_barrier((*sent, near))
-        *sent, acc, highest, sums = lax.optimization_barrier((*sent, *carry))
+        acc, highest, sums = carry
+        *sent, sums = lax.optimization_barrier((*sent, sums))
         carry = (band_rate, acc, highest, sums)
         pending, offsets = sent, ([-step, step] if both else [-step])
     where = describe(offsets[0])
     before, total = call(
         last_states_kernel, [band_shape] * 2, [smem()] + vmem(3), 1_000_000, 500_000
     )(where, pending[0][layers * rows :], sums, band_rate)
+    late, _ = lax.optimization_barrier((gated, total))
+    near = call(near_kernel, wide, vmem(3), 4_000_000_000, 4_000_000)(late, rate_row, res_row)
     attn_out = attend(pending, offsets, (acc, highest), last=True).reshape(rows, heads, size)
 
     totals = [

time: 104 us -> 109 us (1.048)
  waiting for transfers between devices: 3.52 us -> 12.3 us
  local copies, waits for them, and re-layouts: 13 us -> 8.58 us
  starting transfers between devices: 64.1 us -> 66.2 us
    ppermute x7, waiting for transfers between devices: 3.5 us -> 9.58 us  [turn(): lax.ppermute(message, 'y', [(y, (y + by) % ring) for y in range(ring)])]
    unnamed x36 -> x28, local copies, waits for them, and re-layouts: 10.7 us -> 6.25 us
    ppermute x3, waiting for transfers between devices: 0.01 us -> 2.74 us  [body(): lax.ppermute(kv, 'zh', [(z, z + s) for z in range(layers - s)])]
    ppermute x3, starting transfers between devices: 14.2 us -> 15.5 us  [body(): lax.ppermute(total, 'zh', [(z, z + s) for z in range(layers - s)])]
  transfers between devices with their start and end apart: 14 -> 14, of which waited for: 3 -> 5; matrix products, arithmetic and copies ran while one was open for 2% -> 1% of each run, Pallas kernels for 18% -> 17%
where the time goes in v3:
time: 109 us
  starting transfers between devices  66.2 us (61%)
  Pallas kernels  20.5 us (19%)
  waiting for transfers between devices  12.3 us (11%)
  local copies, waits for them, and re-layouts  8.58 us (8%)
    ppermute x7, starting transfers between devices, turn(): lax.ppermute(message, 'y', [(y, (y + by) % ring) for y in range(ring)])  24.9 us
    ppermute x3, starting transfers between devices, body(): lax.ppermute(kv, 'zh', [(z, z + s) for z in range(layers - s)])  22.2 us
    ppermute x3, starting transfers between devices, body(): lax.ppermute(total, 'zh', [(z, z + s) for z in range(layers - s)])  15.5 us
    pallas_call x5, Pallas kernels, attend(): call(functools.partial(attend_kernel, first, last, rows, layers, scale),...  13.9 us
    ppermute x7, waiting for transfers between devices, turn(): lax.ppermute(message, 'y', [(y, (y + by) % ring) for y in range(ring)])  9.58 us
    unnamed x28, local copies, waits for them, and re-layouts  6.25 us
    ppermute x1, starting transfers between devices, body(): lax.ppermute(by_kind[:, rows - 8:], ('zh', 'y'), [(i, i + 1) for i in ran...  3.47 us
    pallas_call x1, Pallas kernels, body(): call(near_kernel, wide, vmem(3), 4000000000, 4000000)  3.39 us
  transfers between devices with their start and end apart: 14, of which 5 were waited for; matrix products, arithmetic and copies ran while one was open for 1% of the time, Pallas kernels for 17%

profile of v3, /device:TPU:6, one launch (start us, length us, event | category | flops | bytes accessed | tf_op | source)
XLA Modules:
  0.0 108.7 jit_solution(3572603464440240115)
XLA Ops:
  0.6 0.8 slice.8
  1.4 3.5 %collective-permute-start = (bf16[3,8,768]{2,1,0:T(8,128)(2,1)S(1)}, bf16[3,8,768]{2,1,0:T(8,128)(2,1)S(1)}, u32[]{:S(2)}, u32[]{:S(2)}) collective-permute-start(bf16[3,8,768]{2,1,0:T(8,128)(2,1)S(1)} %slice.8), channel_id=1, source_target_pairs={{0,6},{6,12},{12,18},{18,24},{24,30},{30,36},{36,42},{42,48},{48,5... | collective-permute-start | bytes 110600 | tf_op jit(solution)/shard_map/ppermute | solution.py:249
  5.0 7.9 %collective-permute-start.1 = (bf16[128,256]{1,0:T(8,128)(2,1)S(1)}, bf16[128,256]{1,0:T(8,128)(2,1)S(1)}, u32[]{:S(2)}, u32[]{:S(2)}) collective-permute-start(bf16[128,256]{1,0:T(8,128)(2,1)S(1)} %get-tuple-element.60), channel_id=1, source_target_pairs={{0,48},{48,96},{96,144},{1,49},{49,97},{97,145},{2,50},{50,98},{98... | collective-permute-start | bytes 196616 | tf_op jit(solution)/shard_map/ppermute | solution.py:245
  12.9 13.0 %collective-permute-start.2 = (bf16[128,256]{1,0:T(8,128)(2,1)S(1)}, bf16[128,256]{1,0:T(8,128)(2,1)S(1)}, u32[]{:S(2)}, u32[]{:S(2)}) collective-permute-start(bf16[128,256]{1,0:T(8,128)(2,1)S(1)} %get-tuple-element.60), channel_id=1, source_target_pairs={{0,96},{48,144},{1,97},{49,145},{2,98},{50,146},{3,99},{51,147},{4... | collective-permute-start | bytes 196616 | tf_op jit(solution)/shard_map/ppermute | solution.py:245
  25.9 1.3 %collective-permute-start.3 = (bf16[128,256]{1,0:T(8,128)(2,1)S(1)}, bf16[128,256]{1,0:T(8,128)(2,1)S(1)}, u32[]{:S(2)}, u32[]{:S(2)}) collective-permute-start(bf16[128,256]{1,0:T(8,128)(2,1)S(1)} %get-tuple-element.60), channel_id=1, source_target_pairs={{0,144},{1,145},{2,146},{3,147},{4,148},{5,149},{6,150},{7,151},{8... | collective-permute-start | bytes 196616 | tf_op jit(solution)/shard_map/ppermute | solution.py:245
  29.1 1.0 shard_map.95
  30.2 2.7 %collective-permute-done.3 = bf16[128,256]{1,0:T(8,128)(2,1)S(1)} collective-permute-done((bf16[128,256]{1,0:T(8,128)(2,1)S(1)}, bf16[128,256]{1,0:T(8,128)(2,1)S(1)}, u32[]{:S(2)}, u32[]{:S(2)}) %collective-permute-start.3) | collective-permute-done | bytes 65568 | tf_op jit(solution)/shard_map/ppermute | solution.py:245
  33.0 3.6 %collective-permute-start.4 = (bf16[608,256]{1,0:T(8,128)(2,1)S(1)}, bf16[608,256]{1,0:T(8,128)(2,1)S(1)}, u32[]{:S(2)}, u32[]{:S(2)}) collective-permute-start(bf16[608,256]{1,0:T(8,128)(2,1)S(1)} %constant_dynamic-update-slice_fusion.refs_0_), channel_id=1, source_target_pairs={{0,6},{6,12},{12,18},{18,24},{24,30},{30,36},{36,42},{42,0},{1,7},... | collective-permute-start | bytes 933896 | tf_op jit(solution)/shard_map/ppermute | solution.py:294
  36.6 3.6 %collective-permute-start.5 = (bf16[608,256]{1,0:T(8,128)(2,1)S(1)}, bf16[608,256]{1,0:T(8,128)(2,1)S(1)}, u32[]{:S(2)}, u32[]{:S(2)}) collective-permute-start(bf16[608,256]{1,0:T(8,128)(2,1)S(1)} %constant_dynamic-update-slice_fusion.refs_0_), channel_id=1, source_target_pairs={{0,42},{6,0},{12,6},{18,12},{24,18},{30,24},{36,30},{42,36},{1,43}... | collective-permute-start | bytes 933896 | tf_op jit(solution)/shard_map/ppermute | solution.py:294
  40.6 1.6 %shard_map.96 = (f32[1024,128]{1,0:T(8,128)S(1)}, f32[1024,128]{1,0:T(8,128)S(1)}, f32[96,256]{1,0:T(8,128)S(1)}) custom-call(s32[8]{0:T(128)S(1)} %concatenate.25.where_ref, bf16[1024,128]{1,0:T(8,128)(2,1)S(1)} %bitcast.30, bf16[608,256]{1,0:T(8,128)(2,1)S(1)} %constant_dynamic-update-slice_fusion.refs_0_, f32[48,256]{1,0:T(8,128)S(1)} %copy.15.refs_1_.refs_2_.rate_ref.refs_3_), custom_call_target="tpu_custom_call" | custom-call | flops 1000000000 | bytes 3000000 | tf_op jit(solution)/shard_map/pallas_call | solution.py:285
  42.2 3.1 %collective-permute-done.4.refs_0_ = bf16[608,256]{1,0:T(8,128)(2,1)S(1)} collective-permute-done((bf16[608,256]{1,0:T(8,128)(2,1)S(1)}, bf16[608,256]{1,0:T(8,128)(2,1)S(1)}, u32[]{:S(2)}, u32[]{:S(2)}) %collective-permute-start.4) | collective-permute-done | bytes 311328 | tf_op jit(solution)/shard_map/ppermute | solution.py:294
  45.3 2.0 %collective-permute-done.5.refs_1_ = bf16[608,256]{1,0:T(8,128)(2,1)S(1)} collective-permute-done((bf16[608,256]{1,0:T(8,128)(2,1)S(1)}, bf16[608,256]{1,0:T(8,128)(2,1)S(1)}, u32[]{:S(2)}, u32[]{:S(2)}) %collective-permute-start.5) | collective-permute-done | bytes 311328 | tf_op jit(solution)/shard_map/ppermute | solution.py:294
  47.3 4.5 %collective-permute-start.6 = (bf16[608,256]{1,0:T(8,128)(2,1)S(1)}, bf16[608,256]{1,0:T(8,128)(2,1)S(1)}, u32[]{:S(2)}, u32[]{:S(2)}) collective-permute-start(bf16[608,256]{1,0:T(8,128)(2,1)S(1)} %collective-permute-done.4.refs_0_), channel_id=1, source_target_pairs={{0,6},{6,12},{12,18},{18,24},{24,30},{30,36},{36,42},{42,0},{1,7},... | collective-permute-start | bytes 933896 | tf_op jit(solution)/shard_map/ppermute | solution.py:294
  51.9 2.5 %collective-permute-start.7 = (bf16[608,256]{1,0:T(8,128)(2,1)S(1)}, bf16[608,256]{1,0:T(8,128)(2,1)S(1)}, u32[]{:S(2)}, u32[]{:S(2)}) collective-permute-start(bf16[608,256]{1,0:T(8,128)(2,1)S(1)} %collective-permute-done.5.refs_1_), channel_id=1, source_target_pairs={{0,42},{6,0},{12,6},{18,12},{24,18},{30,24},{36,30},{42,36},{1,43}... | collective-permute-start | bytes 933896 | tf_op jit(solution)/shard_map/ppermute | solution.py:294
  54.5 2.9 %shard_map.97 = (f32[1024,128]{1,0:T(8,128)S(1)}, f32[1024,128]{1,0:T(8,128)S(1)}, f32[96,256]{1,0:T(8,128)S(1)}) custom-call(s32[16]{0:T(128)S(1)} %concatenate.26.where_ref, bf16[1024,128]{1,0:T(8,128)(2,1)S(1)} %bitcast.31, bf16[608,256]{1,0:T(8,128)(2,1)S(1)} %collective-permute-done.4.refs_0_, bf16[608,256]{1,0:T(8,128)(2,1)S(1)} %collective-permute-done.5.refs_1_, ...), custom_call_target="tpu_custom_call" | custom-call | flops 2000000000 | bytes 3000000 | tf_op jit(solution)/shard_map/pallas_call | solution.py:285
  57.5 0.8 copy-done.2
  58.3 0.8 copy-done.4
  59.1 2.7 %collective-permute-done.7.refs_1_ = bf16[608,256]{1,0:T(8,128)(2,1)S(1)} collective-permute-done((bf16[608,256]{1,0:T(8,128)(2,1)S(1)}, bf16[608,256]{1,0:T(8,128)(2,1)S(1)}, u32[]{:S(2)}, u32[]{:S(2)}) %collective-permute-start.7) | collective-permute-done | bytes 311328 | tf_op jit(solution)/shard_map/ppermute | solution.py:294
  61.7 3.5 %collective-permute-start.8 = (bf16[608,256]{1,0:T(8,128)(2,1)S(1)}, bf16[608,256]{1,0:T(8,128)(2,1)S(1)}, u32[]{:S(2)}, u32[]{:S(2)}) collective-permute-start(bf16[608,256]{1,0:T(8,128)(2,1)S(1)} %collective-permute-done.6.refs_0_), channel_id=1, source_target_pairs={{0,6},{6,12},{12,18},{18,24},{24,30},{30,36},{36,42},{42,0},{1,7},... | collective-permute-start | bytes 933896 | tf_op jit(solution)/shard_map/ppermute | solution.py:294
  65.2 3.6 %collective-permute-start.9 = (bf16[608,256]{1,0:T(8,128)(2,1)S(1)}, bf16[608,256]{1,0:T(8,128)(2,1)S(1)}, u32[]{:S(2)}, u32[]{:S(2)}) collective-permute-start(bf16[608,256]{1,0:T(8,128)(2,1)S(1)} %collective-permute-done.7.refs_1_), channel_id=1, source_target_pairs={{0,42},{6,0},{12,6},{18,12},{24,18},{30,24},{36,30},{42,36},{1,43}... | collective-permute-start | bytes 933896 | tf_op jit(solution)/shard_map/ppermute | solution.py:294
  68.9 1.0 copy-done.3
  70.0 1.0 copy-done.5
  71.0 2.9 %shard_map.98 = (f32[1024,128]{1,0:T(8,128)S(1)}, f32[1024,128]{1,0:T(8,128)S(1)}, f32[96,256]{1,0:T(8,128)S(1)}) custom-call(s32[16]{0:T(128)S(1)} %concatenate.27.where_ref, bf16[1024,128]{1,0:T(8,128)(2,1)S(1)} %bitcast.32, bf16[608,256]{1,0:T(8,128)(2,1)S(1)} %collective-permute-done.6.refs_0_, bf16[608,256]{1,0:T(8,128)(2,1)S(1)} %collective-permute-done.7.refs_1_, ...), custom_call_target="tpu_custom_call" | custom-call | flops 2000000000 | bytes 3000000 | tf_op jit(solution)/shard_map/pallas_call | solution.py:285
  74.0 3.6 %collective-permute-start.10 = (bf16[608,256]{1,0:T(8,128)(2,1)S(1)}, bf16[608,256]{1,0:T(8,128)(2,1)S(1)}, u32[]{:S(2)}, u32[]{:S(2)}) collective-permute-start(bf16[608,256]{1,0:T(8,128)(2,1)S(1)} %collective-permute-done.8.refs_0_), channel_id=1, source_target_pairs={{0,6},{6,12},{12,18},{18,24},{24,30},{30,36},{36,42},{42,0},{1,7},... | collective-permute-start | bytes 933896 | tf_op jit(solution)/shard_map/ppermute | solution.py:294
  79.3 3.0 %shard_map.99 = (f32[1024,128]{1,0:T(8,128)S(1)}, f32[1024,128]{1,0:T(8,128)S(1)}, f32[96,256]{1,0:T(8,128)S(1)}) custom-call(s32[16]{0:T(128)S(1)} %concatenate.28.where_ref, bf16[1024,128]{1,0:T(8,128)(2,1)S(1)} %bitcast.33, bf16[608,256]{1,0:T(8,128)(2,1)S(1)} %collective-permute-done.8.refs_0_, bf16[608,256]{1,0:T(8,128)(2,1)S(1)} %collective-permute-done.9.refs_1_, ...), custom_call_target="tpu_custom_call" | custom-call | flops 2000000000 | bytes 3000000 | tf_op jit(solution)/shard_map/pallas_call | solution.py:285
  82.3 1.7 %collective-permute-done.10.refs_0_ = bf16[608,256]{1,0:T(8,128)(2,1)S(1)} collective-permute-done((bf16[608,256]{1,0:T(8,128)(2,1)S(1)}, bf16[608,256]{1,0:T(8,128)(2,1)S(1)}, u32[]{:S(2)}, u32[]{:S(2)}) %collective-permute-start.10) | collective-permute-done | bytes 311328 | tf_op jit(solution)/shard_map/ppermute | solution.py:294
  84.6 1.3 %collective-permute-start.11 = (f32[48,256]{1,0:T(8,128)S(1)}, f32[48,256]{1,0:T(8,128)S(1)}, u32[]{:S(2)}, u32[]{:S(2)}) collective-permute-start(f32[48,256]{1,0:T(8,128)S(1)} %get-tuple-element.55), channel_id=1, source_target_pairs={{0,48},{48,96},{96,144},{1,49},{49,97},{97,145},{2,50},{50,98},{98... | collective-permute-start | bytes 147464 | tf_op jit(solution)/shard_map/ppermute | solution.py:315
  85.9 12.8 %collective-permute-start.12 = (f32[48,256]{1,0:T(8,128)S(1)}, f32[48,256]{1,0:T(8,128)S(1)}, u32[]{:S(2)}, u32[]{:S(2)}) collective-permute-start(f32[48,256]{1,0:T(8,128)S(1)} %get-tuple-element.55), channel_id=1, source_target_pairs={{0,96},{48,144},{1,97},{49,145},{2,98},{50,146},{3,99},{51,147},{4... | collective-permute-start | bytes 147464 | tf_op jit(solution)/shard_map/ppermute | solution.py:315
  98.7 1.5 %collective-permute-start.13 = (f32[48,256]{1,0:T(8,128)S(1)}, f32[48,256]{1,0:T(8,128)S(1)}, u32[]{:S(2)}, u32[]{:S(2)}) collective-permute-start(f32[48,256]{1,0:T(8,128)S(1)} %get-tuple-element.55), channel_id=1, source_target_pairs={{0,144},{1,145},{2,146},{3,147},{4,148},{5,149},{6,150},{7,151},{8... | collective-permute-start | bytes 147464 | tf_op jit(solution)/shard_map/ppermute | solution.py:315
  100.2 3.4 %shard_map.101.near_ref = f32[128,768]{1,0:T(8,128)S(1)} custom-call(bf16[128,768]{1,0:T(8,128)(2,1)S(1)} %get-tuple-element.56.gated_ref, f32[1,768]{1,0:T(1,128)S(1)} %reshape.52.rate_ref.refs_4_, f32[1,768]{1,0:T(1,128)S(1)} %reshape.57.res_ref.refs_5_), custom_call_target="tpu_custom_call" | custom-call | flops 4000000000 | bytes 4000000 | tf_op jit(solution)/shard_map/pallas_call | solution.py:311
  103.6 3.5 %shard_map.103 = bf16[1024,128]{1,0:T(8,128)(2,1)} custom-call(s32[8]{0:T(128)S(1)} %concatenate.22.where_ref, bf16[1024,128]{1,0:T(8,128)(2,1)S(1)} %bitcast.34, bf16[608,256]{1,0:T(8,128)(2,1)S(1)} %collective-permute-done.10.refs_0_, f32[1024,128]{1,0:T(8,128)S(1)} %get-tuple-element.58.refs_1_, f32[1024,128]{1,0:T(8,128)S(1)} %get-tuple-element.59.refs_2_), custom_call_target="tpu_custom_call" | custom-call | flops 1000000000 | bytes 3000000 | tf_op jit(solution)/shard_map/pallas_call | solution.py:285
  107.1 1.6 %shard_map.102 = bf16[128,768]{1,0:T(8,128)(2,1)} custom-call(s32[8]{0:T(128)S(1)} %concatenate.22.where_ref, f32[128,768]{1,0:T(8,128)S(1)} %get-tuple-element.31.first_ref, bf16[128,768]{1,0:T(8,128)(2,1)S(1)} %get-tuple-element.56.gated_ref, f32[128,768]{1,0:T(8,128)S(1)} %shard_map.101.near_ref, f32[48,256]{1,0:T(8,128)S(1)} %get-tuple-element.57.before_ref, ...), custom_call_target="tpu_custom_call" | custom-call | flops 500000000 | bytes 2000000 | tf_op jit(solution)/shard_map/pallas_call | solution.py:317
  (56 shorter events, 4.8 us)
Async XLA Ops:
  0.6 4.3 %copy-start.7 = (bf16[128,1,128]{2,0,1:T(8,128)(2,1)S(1)}, bf16[128,1,128]{2,0,1:T(8,128)(2,1)}, u32[]{:S(2)}) copy-start(bf16[128,1,128]{2,0,1:T(8,128)(2,1)} %param.15) | copy-start | bytes 98308
  0.6 4.3 %copy-start.8 = (bf16[128,1,128]{2,0,1:T(8,128)(2,1)S(1)}, bf16[128,1,128]{2,0,1:T(8,128)(2,1)}, u32[]{:S(2)}) copy-start(bf16[128,1,128]{2,0,1:T(8,128)(2,1)} %param.14) | copy-start | bytes 98308
  1.4 27.1 %collective-permute-start = (bf16[3,8,768]{2,1,0:T(8,128)(2,1)S(1)}, bf16[3,8,768]{2,1,0:T(8,128)(2,1)S(1)}, u32[]{:S(2)}, u32[]{:S(2)}) collective-permute-start(bf16[3,8,768]{2,1,0:T(8,128)(2,1)S(1)} %slice.8), channel_id=1, source_target_pairs={{0,6},{6,12},{12,18},{18,24},{24,30},{30,36},{36,42},{42,48},{48,5... | collective-permute-start | bytes 110600 | tf_op jit(solution)/shard_map/ppermute | solution.py:249
  4.9 22.3 %copy-start.6 = (f32[16,48]{1,0:T(8,128)S(1)}, f32[16,48]{1,0:T(8,128)}, u32[]{:S(2)}) copy-start(f32[16,48]{1,0:T(8,128)} %param.11) | copy-start | bytes 9220
  5.0 25.2 %collective-permute-start.1 = (bf16[128,256]{1,0:T(8,128)(2,1)S(1)}, bf16[128,256]{1,0:T(8,128)(2,1)S(1)}, u32[]{:S(2)}, u32[]{:S(2)}) collective-permute-start(bf16[128,256]{1,0:T(8,128)(2,1)S(1)} %get-tuple-element.60), channel_id=1, source_target_pairs={{0,48},{48,96},{96,144},{1,49},{49,97},{97,145},{2,50},{50,98},{98... | collective-permute-start | bytes 196616 | tf_op jit(solution)/shard_map/ppermute | solution.py:245
  12.9 17.3 %collective-permute-start.2 = (bf16[128,256]{1,0:T(8,128)(2,1)S(1)}, bf16[128,256]{1,0:T(8,128)(2,1)S(1)}, u32[]{:S(2)}, u32[]{:S(2)}) collective-permute-start(bf16[128,256]{1,0:T(8,128)(2,1)S(1)} %get-tuple-element.60), channel_id=1, source_target_pairs={{0,96},{48,144},{1,97},{49,145},{2,98},{50,146},{3,99},{51,147},{4... | collective-permute-start | bytes 196616 | tf_op jit(solution)/shard_map/ppermute | solution.py:245
  25.9 7.0 %collective-permute-start.3 = (bf16[128,256]{1,0:T(8,128)(2,1)S(1)}, bf16[128,256]{1,0:T(8,128)(2,1)S(1)}, u32[]{:S(2)}, u32[]{:S(2)}) collective-permute-start(bf16[128,256]{1,0:T(8,128)(2,1)S(1)} %get-tuple-element.60), channel_id=1, source_target_pairs={{0,144},{1,145},{2,146},{3,147},{4,148},{5,149},{6,150},{7,151},{8... | collective-permute-start | bytes 196616 | tf_op jit(solution)/shard_map/ppermute | solution.py:245
  27.3 0.7 copy-start.9
  28.0 1.1 copy-start
  32.9 7.7 %copy-start.1 = (bf16[128,8,128]{2,1,0:T(8,128)(2,1)S(1)}, bf16[128,8,128]{2,1,0:T(8,128)(2,1)}, u32[]{:S(2)}) copy-start(bf16[128,8,128]{2,1,0:T(8,128)(2,1)} %param.13) | copy-start | bytes 786436
  33.0 12.4 %collective-permute-start.4 = (bf16[608,256]{1,0:T(8,128)(2,1)S(1)}, bf16[608,256]{1,0:T(8,128)(2,1)S(1)}, u32[]{:S(2)}, u32[]{:S(2)}) collective-permute-start(bf16[608,256]{1,0:T(8,128)(2,1)S(1)} %constant_dynamic-update-slice_fusion.refs_0_), channel_id=1, source_target_pairs={{0,6},{6,12},{12,18},{18,24},{24,30},{30,36},{36,42},{42,0},{1,7},... | collective-permute-start | bytes 933896 | tf_op jit(solution)/shard_map/ppermute | solution.py:294
  36.6 10.8 %collective-permute-start.5 = (bf16[608,256]{1,0:T(8,128)(2,1)S(1)}, bf16[608,256]{1,0:T(8,128)(2,1)S(1)}, u32[]{:S(2)}, u32[]{:S(2)}) collective-permute-start(bf16[608,256]{1,0:T(8,128)(2,1)S(1)} %constant_dynamic-update-slice_fusion.refs_0_), channel_id=1, source_target_pairs={{0,42},{6,0},{12,6},{18,12},{24,18},{30,24},{36,30},{42,36},{1,43}... | collective-permute-start | bytes 933896 | tf_op jit(solution)/shard_map/ppermute | solution.py:294
  47.3 11.8 %collective-permute-start.6 = (bf16[608,256]{1,0:T(8,128)(2,1)S(1)}, bf16[608,256]{1,0:T(8,128)(2,1)S(1)}, u32[]{:S(2)}, u32[]{:S(2)}) collective-permute-start(bf16[608,256]{1,0:T(8,128)(2,1)S(1)} %collective-permute-done.4.refs_0_), channel_id=1, source_target_pairs={{0,6},{6,12},{12,18},{18,24},{24,30},{30,36},{36,42},{42,0},{1,7},... | collective-permute-start | bytes 933896 | tf_op jit(solution)/shard_map/ppermute | solution.py:294
  51.9 9.9 %collective-permute-start.7 = (bf16[608,256]{1,0:T(8,128)(2,1)S(1)}, bf16[608,256]{1,0:T(8,128)(2,1)S(1)}, u32[]{:S(2)}, u32[]{:S(2)}) collective-permute-start(bf16[608,256]{1,0:T(8,128)(2,1)S(1)} %collective-permute-done.5.refs_1_), channel_id=1, source_target_pairs={{0,42},{6,0},{12,6},{18,12},{24,18},{30,24},{36,30},{42,36},{1,43}... | collective-permute-start | bytes 933896 | tf_op jit(solution)/shard_map/ppermute | solution.py:294
  57.5 0.8 copy-start.2
  58.3 0.8 copy-start.4
  61.7 12.2 %collective-permute-start.8 = (bf16[608,256]{1,0:T(8,128)(2,1)S(1)}, bf16[608,256]{1,0:T(8,128)(2,1)S(1)}, u32[]{:S(2)}, u32[]{:S(2)}) collective-permute-start(bf16[608,256]{1,0:T(8,128)(2,1)S(1)} %collective-permute-done.6.refs_0_), channel_id=1, source_target_pairs={{0,6},{6,12},{12,18},{18,24},{24,30},{30,36},{36,42},{42,0},{1,7},... | collective-permute-start | bytes 933896 | tf_op jit(solution)/shard_map/ppermute | solution.py:294
  65.2 8.8 %collective-permute-start.9 = (bf16[608,256]{1,0:T(8,128)(2,1)S(1)}, bf16[608,256]{1,0:T(8,128)(2,1)S(1)}, u32[]{:S(2)}, u32[]{:S(2)}) collective-permute-start(bf16[608,256]{1,0:T(8,128)(2,1)S(1)} %collective-permute-done.7.refs_1_), channel_id=1, source_target_pairs={{0,42},{6,0},{12,6},{18,12},{24,18},{30,24},{36,30},{42,36},{1,43}... | collective-permute-start | bytes 933896 | tf_op jit(solution)/shard_map/ppermute | solution.py:294
  68.9 1.0 copy-start.3
  70.0 1.0 copy-start.5
  74.0 10.0 %collective-permute-start.10 = (bf16[608,256]{1,0:T(8,128)(2,1)S(1)}, bf16[608,256]{1,0:T(8,128)(2,1)S(1)}, u32[]{:S(2)}, u32[]{:S(2)}) collective-permute-start(bf16[608,256]{1,0:T(8,128)(2,1)S(1)} %collective-permute-done.8.refs_0_), channel_id=1, source_target_pairs={{0,6},{6,12},{12,18},{18,24},{24,30},{30,36},{36,42},{42,0},{1,7},... | collective-permute-start | bytes 933896 | tf_op jit(solution)/shard_map/ppermute | solution.py:294
  77.7 0.7 copy-start.10
  78.5 0.7 copy-start.11
  84.6 22.4 %collective-permute-start.11 = (f32[48,256]{1,0:T(8,128)S(1)}, f32[48,256]{1,0:T(8,128)S(1)}, u32[]{:S(2)}, u32[]{:S(2)}) collective-permute-start(f32[48,256]{1,0:T(8,128)S(1)} %get-tuple-element.55), channel_id=1, source_target_pairs={{0,48},{48,96},{96,144},{1,49},{49,97},{97,145},{2,50},{50,98},{98... | collective-permute-start | bytes 147464 | tf_op jit(solution)/shard_map/ppermute | solution.py:315
  85.9 21.2 %collective-permute-start.12 = (f32[48,256]{1,0:T(8,128)S(1)}, f32[48,256]{1,0:T(8,128)S(1)}, u32[]{:S(2)}, u32[]{:S(2)}) collective-permute-start(f32[48,256]{1,0:T(8,128)S(1)} %get-tuple-element.55), channel_id=1, source_target_pairs={{0,96},{48,144},{1,97},{49,145},{2,98},{50,146},{3,99},{51,147},{4... | collective-permute-start | bytes 147464 | tf_op jit(solution)/shard_map/ppermute | solution.py:315
  98.7 8.4 %collective-permute-start.13 = (f32[48,256]{1,0:T(8,128)S(1)}, f32[48,256]{1,0:T(8,128)S(1)}, u32[]{:S(2)}, u32[]{:S(2)}) collective-permute-start(f32[48,256]{1,0:T(8,128)S(1)} %get-tuple-element.55), channel_id=1, source_target_pairs={{0,144},{1,145},{2,146},{3,147},{4,148},{5,149},{6,150},{7,151},{8... | collective-permute-start | bytes 147464 | tf_op jit(solution)/shard_map/ppermute | solution.py:315

commit v4 on v3

--- a/solution.py
+++ b/solution.py
@@ -121,15 +121,29 @@
 
 def gather_states(where_ref, base, message, rate_ref, before, total):
     half = rate_ref.shape[0]
-    states = (message[:half, :], message[half:, :])
+    own = (message[:half, :], message[half : 2 * half, :])
+    older = (message[2 * half : 3 * half, :], message[3 * half :, :])
     place, origin, ring = where_ref[base + 4], where_ref[base + 5], where_ref[base + 6]
     span = where_ref[base + 7].astype(F32)
     rate = -rate_ref[...] * span
     lag = jnp.maximum(place - 1 - origin, 0).astype(F32)
     here = jnp.where(origin < place, 1.0, 0.0)
-    before = before + here * fold(states, rate, lag)
-    total = total + fold(states, rate, (ring - 1 - origin).astype(F32))
+    before = before + here * fold(own, rate, lag)
+    total = total + fold(older, rate, (ring - 1 - origin).astype(F32))
     return before, total
+
+
+def layers_kernel(where_ref, rate_ref, *refs):
+    *states, out_ref = refs
+    half = rate_ref.shape[0]
+    rate = -rate_ref[...] * where_ref[7].astype(F32)
+    total = jnp.zeros(rate_ref.shape, F32)
+    for number, state in enumerate(states):
+        pair = (state[:half, :], state[half:, :])
+        total = total + fold(pair, rate, (number * where_ref[6]).astype(F32))
+    high, low = split(total)
+    out_ref[:half, :] = high
+    out_ref[half:, :] = low
 
 
 def last_states_kernel(where_ref, message_ref, sums_ref, rate_ref, before_ref, total_ref):
@@ -144,15 +158,13 @@
 def join_kernel(
     where_ref, first_ref, gated_ref, near_ref, before_ref, *refs
 ):
-    *totals, band_ref, rate_ref, res_ref, gain_ref, out_ref, past_ref = refs
+    total_ref, band_ref, rate_ref, res_ref, gain_ref, out_ref, past_ref = refs
     rows, width = gated_ref.shape
     modes = GSIZE
     span = where_ref[7].astype(F32)
     band_rate = -band_ref[...] * span
-    past_ref[...] = before_ref[...]
-    for number, total in enumerate(totals):
-        lag = (where_ref[4] + number * where_ref[6]).astype(F32)
-        past_ref[...] += jnp.exp(band_rate * lag) * total[...]
+    lag = where_ref[4].astype(F32)
+    past_ref[...] = before_ref[...] + jnp.exp(band_rate * lag) * total_ref[...]
     row = iota((rows, LANES), 0).astype(F32)
     same = iota((LANES, LANES), 0) // GSIZE == iota((LANES, LANES), 1) // GSIZE
     for tile in range(width // LANES):
@@ -293,7 +305,15 @@
     def turn(message, by):
         return lax.ppermute(message, "y", [(y, (y + by) % ring) for y in range(ring)])
 
-    message = jnp.concatenate(held + [state], axis=0)
+    states = [
+        lax.ppermute(state, "zh", [(z, z + s) for z in range(layers - s)]) for s in range(1, layers)
+    ]
+    near = call(near_kernel, wide, vmem(3), 4_000_000_000, 4_000_000)(gated, rate_row, res_row)
+    *states, near = lax.optimization_barrier((*states, near))
+    older = call(
+        layers_kernel, jax.ShapeDtypeStruct(state.shape, BF16), [smem()] + vmem(layers), 1_000_000, 500_000
+    )(describe(0), band_rate, *states)
+    message = jnp.concatenate(held + [state, older], axis=0)
     pending, offsets, carry = [message], [0], (band_rate,)
     for step in range(1, ring // 2 + 1):
         both = 2 * step < ring
@@ -307,21 +327,16 @@
     before, total = call(
         last_states_kernel, [band_shape] * 2, [smem()] + vmem(3), 1_000_000, 500_000
     )(where, pending[0][layers * rows :], sums, band_rate)
-    late, _ = lax.optimization_barrier((gated, total))
-    near = call(near_kernel, wide, vmem(3), 4_000_000_000, 4_000_000)(late, rate_row, res_row)
     attn_out = attend(pending, offsets, (acc, highest), last=True).reshape(rows, heads, size)
 
-    totals = [
-        lax.ppermute(total, "zh", [(z, z + s) for z in range(layers - s)]) for s in range(1, layers)
-    ]
     hyena_out = call(
         join_kernel,
         jax.ShapeDtypeStruct((rows, width), BF16),
-        [smem()] + vmem(8 + len(totals)),
+        [smem()] + vmem(9),
         500_000_000,
         2_000_000,
         [pltpu.VMEM((bands * modes, 2 * LANES), F32)],
-    )(where, first, gated, near, before, *totals, band_rate, rate_row, res_row, skip_gain.reshape(1, width))
+    )(where, first, gated, near, before, total, band_rate, rate_row, res_row, skip_gain.reshape(1, width))
     return hyena_out, attn_out
 
 

time: 109 us -> 109 us (level)
  the two profiles are of different devices: /device:TPU:6 before, /device:TPU:130 now
where the time goes in v4:
time: 109 us; the launch traced here: 108 us
  starting transfers between devices  58.8 us (54%)
  Pallas kernels  20.7 us (19%)
  local copies, waits for them, and re-layouts  15.7 us (14%)
  waiting for transfers between devices  11.2 us (10%)
  between operations  1.12 us (1%)
    ppermute x7, starting transfers between devices, turn(): lax.ppermute(message, 'y', [(y, (y + by) % ring) for y in range(ring)])  23.7 us
    ppermute x3, starting transfers between devices, body(): lax.ppermute(kv, 'zh', [(z, z + s) for z in range(layers - s)])  19.2 us
    pallas_call x5, Pallas kernels, attend(): call(functools.partial(attend_kernel, first, last, rows, layers, scale),...  13.6 us
    unnamed x41, local copies, waits for them, and re-layouts  13.4 us
    ppermute x3, starting transfers between devices, body(): lax.ppermute(state, 'zh', [(z, z + s) for z in range(layers - s)])  12.4 us
    ppermute x7, waiting for transfers between devices, turn(): lax.ppermute(message, 'y', [(y, (y + by) % ring) for y in range(ring)])  9.55 us
    ppermute x1, starting transfers between devices, body(): lax.ppermute(by_kind[:, rows - 8:], ('zh', 'y'), [(i, i + 1) for i in ran...  3.47 us
    pallas_call x1, Pallas kernels, body(): call(near_kernel, wide, vmem(3), 4000000000, 4000000)  3.39 us
  transfers between devices with their start and end apart: 14, of which 5 were waited for; matrix products, arithmetic and copies ran while one was open for 2% of the time, Pallas kernels for 13%

profile of v4, /device:TPU:130, one launch (start us, length us, event | category | flops | bytes accessed | tf_op | source)
XLA Modules:
  0.0 108.3 jit_solution(10940519989453183743)
XLA Ops:
  1.4 9.1 %collective-permute-start.4 = (bf16[128,256]{1,0:T(8,128)(2,1)S(1)}, bf16[128,256]{1,0:T(8,128)(2,1)S(1)}, u32[]{:S(2)}, u32[]{:S(2)}) collective-permute-start(bf16[128,256]{1,0:T(8,128)(2,1)S(1)} %get-tuple-element.66), channel_id=1, source_target_pairs={{0,48},{48,96},{96,144},{1,49},{49,97},{97,145},{2,50},{50,98},{98... | collective-permute-start | bytes 196616 | tf_op jit(solution)/shard_map/ppermute | solution.py:257
  10.5 8.8 %collective-permute-start.5 = (bf16[128,256]{1,0:T(8,128)(2,1)S(1)}, bf16[128,256]{1,0:T(8,128)(2,1)S(1)}, u32[]{:S(2)}, u32[]{:S(2)}) collective-permute-start(bf16[128,256]{1,0:T(8,128)(2,1)S(1)} %get-tuple-element.66), channel_id=1, source_target_pairs={{0,96},{48,144},{1,97},{49,145},{2,98},{50,146},{3,99},{51,147},{4... | collective-permute-start | bytes 196616 | tf_op jit(solution)/shard_map/ppermute | solution.py:257
  19.4 1.3 %collective-permute-start.6 = (bf16[128,256]{1,0:T(8,128)(2,1)S(1)}, bf16[128,256]{1,0:T(8,128)(2,1)S(1)}, u32[]{:S(2)}, u32[]{:S(2)}) collective-permute-start(bf16[128,256]{1,0:T(8,128)(2,1)S(1)} %get-tuple-element.66), channel_id=1, source_target_pairs={{0,144},{1,145},{2,146},{3,147},{4,148},{5,149},{6,150},{7,151},{8... | collective-permute-start | bytes 196616 | tf_op jit(solution)/shard_map/ppermute | solution.py:257
  21.4 3.5 %collective-permute-start = (bf16[3,8,768]{2,1,0:T(8,128)(2,1)S(1)}, bf16[3,8,768]{2,1,0:T(8,128)(2,1)S(1)}, u32[]{:S(2)}, u32[]{:S(2)}) collective-permute-start(bf16[3,8,768]{2,1,0:T(8,128)(2,1)S(1)} %slice.8), channel_id=1, source_target_pairs={{0,6},{6,12},{12,18},{18,24},{24,30},{30,36},{36,42},{42,48},{48,5... | collective-permute-start | bytes 110600 | tf_op jit(solution)/shard_map/ppermute | solution.py:261
  27.8 1.0 shard_map.95
  28.8 7.5 %collective-permute-start.1 = (bf16[96,256]{1,0:T(8,128)(2,1)S(1)}, bf16[96,256]{1,0:T(8,128)(2,1)S(1)}, u32[]{:S(2)}, u32[]{:S(2)}) collective-permute-start(bf16[96,256]{1,0:T(8,128)(2,1)S(1)} %get-tuple-element.36), channel_id=1, source_target_pairs={{0,48},{48,96},{96,144},{1,49},{49,97},{97,145},{2,50},{50,98},{98... | collective-permute-start | bytes 147464 | tf_op jit(solution)/shard_map/ppermute | solution.py:309
  36.4 3.6 %collective-permute-start.2 = (bf16[96,256]{1,0:T(8,128)(2,1)S(1)}, bf16[96,256]{1,0:T(8,128)(2,1)S(1)}, u32[]{:S(2)}, u32[]{:S(2)}) collective-permute-start(bf16[96,256]{1,0:T(8,128)(2,1)S(1)} %get-tuple-element.36), channel_id=1, source_target_pairs={{0,96},{48,144},{1,97},{49,145},{2,98},{50,146},{3,99},{51,147},{4... | collective-permute-start | bytes 147464 | tf_op jit(solution)/shard_map/ppermute | solution.py:309
  39.9 3.4 %shard_map.96.near_ref = f32[128,768]{1,0:T(8,128)S(1)} custom-call(bf16[128,768]{1,0:T(8,128)(2,1)S(1)} %get-tuple-element.35.gated_ref, f32[1,768]{1,0:T(1,128)S(1)} %reshape.52.rate_ref.refs_2_, f32[1,768]{1,0:T(1,128)S(1)} %reshape.53.res_ref.refs_3_), custom_call_target="tpu_custom_call" | custom-call | flops 4000000000 | bytes 4000000 | tf_op jit(solution)/shard_map/pallas_call | solution.py:311
  43.3 1.3 %collective-permute-start.3 = (bf16[96,256]{1,0:T(8,128)(2,1)S(1)}, bf16[96,256]{1,0:T(8,128)(2,1)S(1)}, u32[]{:S(2)}, u32[]{:S(2)}) collective-permute-start(bf16[96,256]{1,0:T(8,128)(2,1)S(1)} %get-tuple-element.36), channel_id=1, source_target_pairs={{0,144},{1,145},{2,146},{3,147},{4,148},{5,149},{6,150},{7,151},{8... | collective-permute-start | bytes 147464 | tf_op jit(solution)/shard_map/ppermute | solution.py:309
  44.7 1.6 %collective-permute-done.3.refs_2_ = bf16[96,256]{1,0:T(8,128)(2,1)S(1)} collective-permute-done((bf16[96,256]{1,0:T(8,128)(2,1)S(1)}, bf16[96,256]{1,0:T(8,128)(2,1)S(1)}, u32[]{:S(2)}, u32[]{:S(2)}) %collective-permute-start.3) | collective-permute-done | bytes 49184 | tf_op jit(solution)/shard_map/ppermute | solution.py:309
  47.0 1.9 %collective-permute-start.7 = (bf16[704,256]{1,0:T(8,128)(2,1)S(1)}, bf16[704,256]{1,0:T(8,128)(2,1)S(1)}, u32[]{:S(2)}, u32[]{:S(2)}) collective-permute-start(bf16[704,256]{1,0:T(8,128)(2,1)S(1)} %constant_dynamic-update-slice_fusion.refs_0_), channel_id=1, source_target_pairs={{0,6},{6,12},{12,18},{18,24},{24,30},{30,36},{36,42},{42,0},{1,7},... | collective-permute-start | bytes 1081352 | tf_op jit(solution)/shard_map/ppermute | solution.py:306
  48.9 5.1 %collective-permute-start.8 = (bf16[704,256]{1,0:T(8,128)(2,1)S(1)}, bf16[704,256]{1,0:T(8,128)(2,1)S(1)}, u32[]{:S(2)}, u32[]{:S(2)}) collective-permute-start(bf16[704,256]{1,0:T(8,128)(2,1)S(1)} %constant_dynamic-update-slice_fusion.refs_0_), channel_id=1, source_target_pairs={{0,42},{6,0},{12,6},{18,12},{24,18},{30,24},{36,30},{42,36},{1,43}... | collective-permute-start | bytes 1081352 | tf_op jit(solution)/shard_map/ppermute | solution.py:306
  54.1 1.6 %shard_map.98 = (f32[1024,128]{1,0:T(8,128)S(1)}, f32[1024,128]{1,0:T(8,128)S(1)}, f32[96,256]{1,0:T(8,128)S(1)}) custom-call(s32[8]{0:T(128)S(1)} %concatenate.25.where_ref, bf16[1024,128]{1,0:T(8,128)(2,1)S(1)} %bitcast.30, bf16[704,256]{1,0:T(8,128)(2,1)S(1)} %constant_dynamic-update-slice_fusion.refs_0_, f32[48,256]{1,0:T(8,128)S(1)} %copy.16.rate_ref.refs_1_.refs_2_), custom_call_target="tpu_custom_call" | custom-call | flops 1000000000 | bytes 3000000 | tf_op jit(solution)/shard_map/pallas_call | solution.py:297
  57.5 2.1 %collective-permute-done.8.refs_1_ = bf16[704,256]{1,0:T(8,128)(2,1)S(1)} collective-permute-done((bf16[704,256]{1,0:T(8,128)(2,1)S(1)}, bf16[704,256]{1,0:T(8,128)(2,1)S(1)}, u32[]{:S(2)}, u32[]{:S(2)}) %collective-permute-start.8) | collective-permute-done | bytes 360480 | tf_op jit(solution)/shard_map/ppermute | solution.py:306
  59.6 5.6 %collective-permute-start.10 = (bf16[704,256]{1,0:T(8,128)(2,1)S(1)}, bf16[704,256]{1,0:T(8,128)(2,1)S(1)}, u32[]{:S(2)}, u32[]{:S(2)}) collective-permute-start(bf16[704,256]{1,0:T(8,128)(2,1)S(1)} %collective-permute-done.8.refs_1_), channel_id=1, source_target_pairs={{0,42},{6,0},{12,6},{18,12},{24,18},{30,24},{36,30},{42,36},{1,43}... | collective-permute-start | bytes 1081352 | tf_op jit(solution)/shard_map/ppermute | solution.py:306
  65.2 1.9 %collective-permute-start.9 = (bf16[704,256]{1,0:T(8,128)(2,1)S(1)}, bf16[704,256]{1,0:T(8,128)(2,1)S(1)}, u32[]{:S(2)}, u32[]{:S(2)}) collective-permute-start(bf16[704,256]{1,0:T(8,128)(2,1)S(1)} %collective-permute-done.7.refs_0_), channel_id=1, source_target_pairs={{0,6},{6,12},{12,18},{18,24},{24,30},{30,36},{36,42},{42,0},{1,7},... | collective-permute-start | bytes 1081352 | tf_op jit(solution)/shard_map/ppermute | solution.py:306
  67.2 1.0 copy-done.3
  68.3 1.0 copy-done.5
  69.3 2.8 %shard_map.99 = (f32[1024,128]{1,0:T(8,128)S(1)}, f32[1024,128]{1,0:T(8,128)S(1)}, f32[96,256]{1,0:T(8,128)S(1)}) custom-call(s32[16]{0:T(128)S(1)} %concatenate.27.where_ref, bf16[1024,128]{1,0:T(8,128)(2,1)S(1)} %bitcast.31, bf16[704,256]{1,0:T(8,128)(2,1)S(1)} %collective-permute-done.7.refs_0_, bf16[704,256]{1,0:T(8,128)(2,1)S(1)} %collective-permute-done.8.refs_1_, ...), custom_call_target="tpu_custom_call" | custom-call | flops 2000000000 | bytes 3000000 | tf_op jit(solution)/shard_map/pallas_call | solution.py:297
  73.7 4.6 %collective-permute-done.9.refs_0_ = bf16[704,256]{1,0:T(8,128)(2,1)S(1)} collective-permute-done((bf16[704,256]{1,0:T(8,128)(2,1)S(1)}, bf16[704,256]{1,0:T(8,128)(2,1)S(1)}, u32[]{:S(2)}, u32[]{:S(2)}) %collective-permute-start.9) | collective-permute-done | bytes 360480 | tf_op jit(solution)/shard_map/ppermute | solution.py:306
  78.4 1.9 %collective-permute-start.11 = (bf16[704,256]{1,0:T(8,128)(2,1)S(1)}, bf16[704,256]{1,0:T(8,128)(2,1)S(1)}, u32[]{:S(2)}, u32[]{:S(2)}) collective-permute-start(bf16[704,256]{1,0:T(8,128)(2,1)S(1)} %collective-permute-done.9.refs_0_), channel_id=1, source_target_pairs={{0,6},{6,12},{12,18},{18,24},{24,30},{30,36},{36,42},{42,0},{1,7},... | collective-permute-start | bytes 1081352 | tf_op jit(solution)/shard_map/ppermute | solution.py:306
  80.3 5.1 %collective-permute-start.12 = (bf16[704,256]{1,0:T(8,128)(2,1)S(1)}, bf16[704,256]{1,0:T(8,128)(2,1)S(1)}, u32[]{:S(2)}, u32[]{:S(2)}) collective-permute-start(bf16[704,256]{1,0:T(8,128)(2,1)S(1)} %collective-permute-done.10.refs_1_), channel_id=1, source_target_pairs={{0,42},{6,0},{12,6},{18,12},{24,18},{30,24},{36,30},{42,36},{1,43}... | collective-permute-start | bytes 1081352 | tf_op jit(solution)/shard_map/ppermute | solution.py:306
  85.5 1.0 copy-done.11
  86.6 1.0 copy-done.13
  87.6 2.9 %shard_map.100 = (f32[1024,128]{1,0:T(8,128)S(1)}, f32[1024,128]{1,0:T(8,128)S(1)}, f32[96,256]{1,0:T(8,128)S(1)}) custom-call(s32[16]{0:T(128)S(1)} %concatenate.28.where_ref, bf16[1024,128]{1,0:T(8,128)(2,1)S(1)} %bitcast.32, bf16[704,256]{1,0:T(8,128)(2,1)S(1)} %collective-permute-done.9.refs_0_, bf16[704,256]{1,0:T(8,128)(2,1)S(1)} %collective-permute-done.10.refs_1_, ...), custom_call_target="tpu_custom_call" | custom-call | flops 2000000000 | bytes 3000000 | tf_op jit(solution)/shard_map/pallas_call | solution.py:297
  92.1 2.1 %collective-permute-start.13 = (bf16[704,256]{1,0:T(8,128)(2,1)S(1)}, bf16[704,256]{1,0:T(8,128)(2,1)S(1)}, u32[]{:S(2)}, u32[]{:S(2)}) collective-permute-start(bf16[704,256]{1,0:T(8,128)(2,1)S(1)} %collective-permute-done.11.refs_0_), channel_id=1, source_target_pairs={{0,6},{6,12},{12,18},{18,24},{24,30},{30,36},{36,42},{42,0},{1,7},... | collective-permute-start | bytes 1081352 | tf_op jit(solution)/shard_map/ppermute | solution.py:306
  95.1 1.0 copy-done.7
  96.2 1.0 copy-done.9
  97.2 2.8 %shard_map.101 = (f32[1024,128]{1,0:T(8,128)S(1)}, f32[1024,128]{1,0:T(8,128)S(1)}, f32[96,256]{1,0:T(8,128)S(1)}) custom-call(s32[16]{0:T(128)S(1)} %concatenate.29.where_ref, bf16[1024,128]{1,0:T(8,128)(2,1)S(1)} %bitcast.33, bf16[704,256]{1,0:T(8,128)(2,1)S(1)} %collective-permute-done.11.refs_0_, bf16[704,256]{1,0:T(8,128)(2,1)S(1)} %collective-permute-done.12.refs_1_, ...), custom_call_target="tpu_custom_call" | custom-call | flops 2000000000 | bytes 3000000 | tf_op jit(solution)/shard_map/pallas_call | solution.py:297
  100.0 2.6 %collective-permute-done.13.refs_0_ = bf16[704,256]{1,0:T(8,128)(2,1)S(1)} collective-permute-done((bf16[704,256]{1,0:T(8,128)(2,1)S(1)}, bf16[704,256]{1,0:T(8,128)(2,1)S(1)}, u32[]{:S(2)}, u32[]{:S(2)}) %collective-permute-start.13) | collective-permute-done | bytes 360480 | tf_op jit(solution)/shard_map/ppermute | solution.py:306
  102.6 3.5 %shard_map.104 = bf16[1024,128]{1,0:T(8,128)(2,1)} custom-call(s32[8]{0:T(128)S(1)} %concatenate.23.where_ref, bf16[1024,128]{1,0:T(8,128)(2,1)S(1)} %bitcast.34, bf16[704,256]{1,0:T(8,128)(2,1)S(1)} %collective-permute-done.13.refs_0_, f32[1024,128]{1,0:T(8,128)S(1)} %get-tuple-element.64.refs_1_, f32[1024,128]{1,0:T(8,128)S(1)} %get-tuple-element.65.refs_2_), custom_call_target="tpu_custom_call" | custom-call | flops 1000000000 | bytes 3000000 | tf_op jit(solution)/shard_map/pallas_call | solution.py:297
  106.7 1.6 %shard_map.103 = bf16[128,768]{1,0:T(8,128)(2,1)} custom-call(s32[8]{0:T(128)S(1)} %concatenate.23.where_ref, f32[128,768]{1,0:T(8,128)S(1)} %get-tuple-element.34.first_ref, bf16[128,768]{1,0:T(8,128)(2,1)S(1)} %get-tuple-element.35.gated_ref, f32[128,768]{1,0:T(8,128)S(1)} %shard_map.96.near_ref, f32[48,256]{1,0:T(8,128)S(1)} %get-tuple-element.62.before_ref, ...), custom_call_target="tpu_custom_call" | custom-call | flops 500000000 | bytes 2000000 | tf_op jit(solution)/shard_map/pallas_call | solution.py:332
  (70 shorter events, 11.7 us)
Async XLA Ops:
  1.4 41.9 %collective-permute-start.4 = (bf16[128,256]{1,0:T(8,128)(2,1)S(1)}, bf16[128,256]{1,0:T(8,128)(2,1)S(1)}, u32[]{:S(2)}, u32[]{:S(2)}) collective-permute-start(bf16[128,256]{1,0:T(8,128)(2,1)S(1)} %get-tuple-element.66), channel_id=1, source_target_pairs={{0,48},{48,96},{96,144},{1,49},{49,97},{97,145},{2,50},{50,98},{98... | collective-permute-start | bytes 196616 | tf_op jit(solution)/shard_map/ppermute | solution.py:257
  10.5 34.1 %collective-permute-start.5 = (bf16[128,256]{1,0:T(8,128)(2,1)S(1)}, bf16[128,256]{1,0:T(8,128)(2,1)S(1)}, u32[]{:S(2)}, u32[]{:S(2)}) collective-permute-start(bf16[128,256]{1,0:T(8,128)(2,1)S(1)} %get-tuple-element.66), channel_id=1, source_target_pairs={{0,96},{48,144},{1,97},{49,145},{2,98},{50,146},{3,99},{51,147},{4... | collective-permute-start | bytes 196616 | tf_op jit(solution)/shard_map/ppermute | solution.py:257
  19.4 25.3 %collective-permute-start.6 = (bf16[128,256]{1,0:T(8,128)(2,1)S(1)}, bf16[128,256]{1,0:T(8,128)(2,1)S(1)}, u32[]{:S(2)}, u32[]{:S(2)}) collective-permute-start(bf16[128,256]{1,0:T(8,128)(2,1)S(1)} %get-tuple-element.66), channel_id=1, source_target_pairs={{0,144},{1,145},{2,146},{3,147},{4,148},{5,149},{6,150},{7,151},{8... | collective-permute-start | bytes 196616 | tf_op jit(solution)/shard_map/ppermute | solution.py:257
  21.4 6.3 %collective-permute-start = (bf16[3,8,768]{2,1,0:T(8,128)(2,1)S(1)}, bf16[3,8,768]{2,1,0:T(8,128)(2,1)S(1)}, u32[]{:S(2)}, u32[]{:S(2)}) collective-permute-start(bf16[3,8,768]{2,1,0:T(8,128)(2,1)S(1)} %slice.8), channel_id=1, source_target_pairs={{0,6},{6,12},{12,18},{18,24},{24,30},{30,36},{36,42},{42,48},{48,5... | collective-permute-start | bytes 110600 | tf_op jit(solution)/shard_map/ppermute | solution.py:261
  24.9 0.7 copy-start.14
  25.8 0.7 copy-start.15
  26.5 0.7 copy-start.16
  26.7 1.1 copy-start
  28.8 15.9 %collective-permute-start.1 = (bf16[96,256]{1,0:T(8,128)(2,1)S(1)}, bf16[96,256]{1,0:T(8,128)(2,1)S(1)}, u32[]{:S(2)}, u32[]{:S(2)}) collective-permute-start(bf16[96,256]{1,0:T(8,128)(2,1)S(1)} %get-tuple-element.36), channel_id=1, source_target_pairs={{0,48},{48,96},{96,144},{1,49},{49,97},{97,145},{2,50},{50,98},{98... | collective-permute-start | bytes 147464 | tf_op jit(solution)/shard_map/ppermute | solution.py:309
  36.4 8.4 %collective-permute-start.2 = (bf16[96,256]{1,0:T(8,128)(2,1)S(1)}, bf16[96,256]{1,0:T(8,128)(2,1)S(1)}, u32[]{:S(2)}, u32[]{:S(2)}) collective-permute-start(bf16[96,256]{1,0:T(8,128)(2,1)S(1)} %get-tuple-element.36), channel_id=1, source_target_pairs={{0,96},{48,144},{1,97},{49,145},{2,98},{50,146},{3,99},{51,147},{4... | collective-permute-start | bytes 147464 | tf_op jit(solution)/shard_map/ppermute | solution.py:309
  43.3 3.0 %collective-permute-start.3 = (bf16[96,256]{1,0:T(8,128)(2,1)S(1)}, bf16[96,256]{1,0:T(8,128)(2,1)S(1)}, u32[]{:S(2)}, u32[]{:S(2)}) collective-permute-start(bf16[96,256]{1,0:T(8,128)(2,1)S(1)} %get-tuple-element.36), channel_id=1, source_target_pairs={{0,144},{1,145},{2,146},{3,147},{4,148},{5,149},{6,150},{7,151},{8... | collective-permute-start | bytes 147464 | tf_op jit(solution)/shard_map/ppermute | solution.py:309
  44.7 9.4 %copy-start.1 = (bf16[128,8,128]{2,1,0:T(8,128)(2,1)S(1)}, bf16[128,8,128]{2,1,0:T(8,128)(2,1)}, u32[]{:S(2)}) copy-start(bf16[128,8,128]{2,1,0:T(8,128)(2,1)} %param.13) | copy-start | bytes 786436
  47.0 10.5 %collective-permute-start.7 = (bf16[704,256]{1,0:T(8,128)(2,1)S(1)}, bf16[704,256]{1,0:T(8,128)(2,1)S(1)}, u32[]{:S(2)}, u32[]{:S(2)}) collective-permute-start(bf16[704,256]{1,0:T(8,128)(2,1)S(1)} %constant_dynamic-update-slice_fusion.refs_0_), channel_id=1, source_target_pairs={{0,6},{6,12},{12,18},{18,24},{24,30},{30,36},{36,42},{42,0},{1,7},... | collective-permute-start | bytes 1081352 | tf_op jit(solution)/shard_map/ppermute | solution.py:306
  48.9 10.7 %collective-permute-start.8 = (bf16[704,256]{1,0:T(8,128)(2,1)S(1)}, bf16[704,256]{1,0:T(8,128)(2,1)S(1)}, u32[]{:S(2)}, u32[]{:S(2)}) collective-permute-start(bf16[704,256]{1,0:T(8,128)(2,1)S(1)} %constant_dynamic-update-slice_fusion.refs_0_), channel_id=1, source_target_pairs={{0,42},{6,0},{12,6},{18,12},{24,18},{30,24},{36,30},{42,36},{1,43}... | collective-permute-start | bytes 1081352 | tf_op jit(solution)/shard_map/ppermute | solution.py:306
  55.6 0.8 copy-start.2
  56.4 0.8 copy-start.4
  59.6 14.2 %collective-permute-start.10 = (bf16[704,256]{1,0:T(8,128)(2,1)S(1)}, bf16[704,256]{1,0:T(8,128)(2,1)S(1)}, u32[]{:S(2)}, u32[]{:S(2)}) collective-permute-start(bf16[704,256]{1,0:T(8,128)(2,1)S(1)} %collective-permute-done.8.refs_1_), channel_id=1, source_target_pairs={{0,42},{6,0},{12,6},{18,12},{24,18},{30,24},{36,30},{42,36},{1,43}... | collective-permute-start | bytes 1081352 | tf_op jit(solution)/shard_map/ppermute | solution.py:306
  65.2 13.2 %collective-permute-start.9 = (bf16[704,256]{1,0:T(8,128)(2,1)S(1)}, bf16[704,256]{1,0:T(8,128)(2,1)S(1)}, u32[]{:S(2)}, u32[]{:S(2)}) collective-permute-start(bf16[704,256]{1,0:T(8,128)(2,1)S(1)} %collective-permute-done.7.refs_0_), channel_id=1, source_target_pairs={{0,6},{6,12},{12,18},{18,24},{24,30},{30,36},{36,42},{42,0},{1,7},... | collective-permute-start | bytes 1081352 | tf_op jit(solution)/shard_map/ppermute | solution.py:306
  67.2 1.0 copy-start.3
  68.3 1.0 copy-start.5
  72.1 0.8 copy-start.10
  72.9 0.8 copy-start.12
  78.4 13.7 %collective-permute-start.11 = (bf16[704,256]{1,0:T(8,128)(2,1)S(1)}, bf16[704,256]{1,0:T(8,128)(2,1)S(1)}, u32[]{:S(2)}, u32[]{:S(2)}) collective-permute-start(bf16[704,256]{1,0:T(8,128)(2,1)S(1)} %collective-permute-done.9.refs_0_), channel_id=1, source_target_pairs={{0,6},{6,12},{12,18},{18,24},{24,30},{30,36},{36,42},{42,0},{1,7},... | collective-permute-start | bytes 1081352 | tf_op jit(solution)/shard_map/ppermute | solution.py:306
  80.3 11.8 %collective-permute-start.12 = (bf16[704,256]{1,0:T(8,128)(2,1)S(1)}, bf16[704,256]{1,0:T(8,128)(2,1)S(1)}, u32[]{:S(2)}, u32[]{:S(2)}) collective-permute-start(bf16[704,256]{1,0:T(8,128)(2,1)S(1)} %collective-permute-done.10.refs_1_), channel_id=1, source_target_pairs={{0,42},{6,0},{12,6},{18,12},{24,18},{30,24},{36,30},{42,36},{1,43}... | collective-permute-start | bytes 1081352 | tf_op jit(solution)/shard_map/ppermute | solution.py:306
  85.5 1.0 copy-start.11
  86.6 1.0 copy-start.13
  90.5 0.8 copy-start.6
  91.3 0.8 copy-start.8
  92.1 10.5 %collective-permute-start.13 = (bf16[704,256]{1,0:T(8,128)(2,1)S(1)}, bf16[704,256]{1,0:T(8,128)(2,1)S(1)}, u32[]{:S(2)}, u32[]{:S(2)}) collective-permute-start(bf16[704,256]{1,0:T(8,128)(2,1)S(1)} %collective-permute-done.11.refs_0_), channel_id=1, source_target_pairs={{0,6},{6,12},{12,18},{18,24},{24,30},{30,36},{36,42},{42,0},{1,7},... | collective-permute-start | bytes 1081352 | tf_op jit(solution)/shard_map/ppermute | solution.py:306
  94.3 0.7 copy-start.17
  95.1 1.0 copy-start.7
  96.2 1.0 copy-start.9
